TPU v7x, 32 devices: a whole 2x2x4 slice. The times are simulated.
32 devices in a mesh: scan: 2 (over x), slab: 16 (over z, y, core).
Axes of the slice: x: 2, y: 2, z: 4, core: 2. Of those that a mesh axis runs over, the one named last changes fastest.
Arguments:
- sinogram: bfloat16 [1024, 8, 128], P(('scan', 'slab')), parts along dimension 0, may hold values from -144 to 144
- start_volume: float32 [512, 8, 128], P(('scan', 'slab')), parts along dimension 0, may hold values from -6 to 6
- slot_voxel: int32 [8192, 4], P(('scan', 'slab')), parts along dimension 0, may hold values from 0 to 15
- slot_ray: int32 [8192], P(('scan', 'slab')), parts along dimension 0, may hold values from 0 to 31
- live_count: int32 [512], P(('scan', 'slab')), parts along dimension 0, may hold values from 0 to 16, as said below
- block_slope: float32 [8192, 4], P(('scan', 'slab')), parts along dimension 0, may hold values from 0.8 to 1.25
- block_offset: float32 [8192, 4], P(('scan', 'slab')), parts along dimension 0, may hold values from -8 to 8
Outputs:
- recon_volume: float32 [512, 8, 128], P(('scan', 'slab')), parts along dimension 0
There are 2 independent parts, one for each index of `scan`. A program takes and returns all parts, laid end to end along the dimension named above; each array names one. Nothing has to cross between parts.
Inputs may be any that keep to these rules, and one draw needn't show every extreme that they name: `live_count`: every device's 16 slots to itself are all live.
All inputs are finite; a program needn't handle non-finite values.
Results may differ from a plain program's by a relative error of at most 0.0039.
Values may be sent and summed in bfloat16 or wider, within the bound.
No kernel may reach another device: no remote copies, remote signals or barrier semaphores. Data moves between devices by JAX's collectives and lax.ppermute only.
A program may use at most 64 MiB of HBM per device.

v0:
```python
import functools

import jax
import jax.numpy as jnp
from jax import lax
from jax.experimental import pallas as pl
from jax.experimental.pallas import tpu as pltpu
from jax.sharding import PartitionSpec as P

ITERS = 2
CHUNK = 16
F32 = jnp.float32
BF16 = jnp.bfloat16
I32 = jnp.int32
HIGHEST = lax.Precision.HIGHEST
VMEM = pl.BlockSpec(memory_space=pltpu.VMEM)
ANY = pl.BlockSpec(memory_space=pl.ANY)
SMEM = pl.BlockSpec(memory_space=pltpu.SMEM)
HBM = pl.BlockSpec(memory_space=pltpu.HBM)


def hat(ray, centre):
    return jnp.maximum(0.0, 1.0 - jnp.abs(ray - centre)).astype(BF16)


def row_taps(offset, slope, extent):
    shape = (offset.shape[0], extent)
    ray = lax.broadcasted_iota(I32, shape, 1).astype(F32)
    inverse = jnp.broadcast_to(1.0 / slope, shape)
    offset = jnp.broadcast_to(offset, shape)
    slope = jnp.broadcast_to(slope, shape)
    middle = jnp.floor((ray - offset) * inverse + 0.5)
    middle = jnp.minimum(jnp.maximum(middle, 1.0), extent - 2.0)
    weights = [hat(ray, offset + slope * (middle + step)) for step in (-1.0, 0.0, 1.0)]
    return middle.astype(I32), weights


def column_taps(offset, slope, extent):
    shape = (offset.shape[0], extent)
    voxel = lax.broadcasted_iota(I32, shape, 1).astype(F32)
    centre = jnp.broadcast_to(offset, shape) + jnp.broadcast_to(slope, shape) * voxel
    first = jnp.minimum(jnp.maximum(jnp.floor(centre), 0.0), extent - 2.0)
    weights = [hat(first + step, centre) for step in (0.0, 1.0)]
    return first.astype(I32), weights


def repeat_rows(values, times):
    return jnp.concatenate(
        [jnp.broadcast_to(values[row:row + 1, :], (times, values.shape[1]))
         for row in range(values.shape[0])], axis=0)


def contract_lanes(left, right):
    return lax.dot_general(
        left.astype(BF16), right.astype(BF16), (((1,), (1,)), ((), ())), preferred_element_type=F32)


def per_slot(live_ref, slots, capacity):
    targets = live_ref.shape[1]
    slot = lax.broadcasted_iota(I32, (targets, slots), 1)
    owner = lax.broadcasted_iota(I32, (targets, slots), 0)
    expand = (lax.div(slot, capacity) == owner).astype(F32)
    return jnp.dot(live_ref[...].astype(F32), expand, precision=HIGHEST, preferred_element_type=F32)


def pack_kernel(capacity, partners, *refs):
    sources, outs, loaded, arrived, packed = refs[:6], refs[6:-8], refs[-8:-2], refs[-2], refs[-1]
    copies = [
        pltpu.make_async_copy(source, ref, arrived.at[place])
        for place, (source, ref) in enumerate(zip(sources, loaded))]
    for copy in copies:
        copy.start()
    for copy in copies:
        copy.wait()
    volume_ref, offset_ref, slope_ref, voxel_ref, ray_ref, live_ref = loaded
    rows, extent = volume_ref.shape
    slots = ray_ref.shape[1]
    fields = []
    for ref in (offset_ref, slope_ref):
        left = ref[...]
        for addend in range(3):
            part = left.astype(BF16).astype(F32)
            fields.append(part)
            left = left - part
    fields.append(voxel_ref[...].astype(F32))
    fields.append(ray_ref[...].astype(F32))
    fields.append(per_slot(live_ref, slots, capacity))
    used = sum(field.shape[0] for field in fields)
    fields.append(jnp.zeros((-used % 16, slots), F32))
    fields = jnp.concatenate(fields, axis=0)
    height = fields.shape[0]
    for part in range(slots // extent):
        at = pl.ds(part * height, height)
        packed[at, :] = fields[:, part * extent:(part + 1) * extent].astype(BF16)
    me = lax.axis_index("slab").astype(I32)
    odd = sum(lax.bitwise_and(lax.shift_right_logical(me, bit), 1) for bit in range(4)) % 2
    for place, out_ref in enumerate(outs):
        out_ref[0:rows, :] = volume_ref[...].astype(BF16)
        if not partners:
            out_ref[rows:, :] = packed[...]
            continue
        distance = jnp.where(odd == 0, partners[place][0], partners[place][1])
        part = lax.div(lax.bitwise_xor(me, distance) * capacity, extent)
        out_ref[rows:, :] = packed[pl.ds(pl.multiple_of(part * height, 16), height), :]


def setup_kernel(n_payloads, members, stride, span, sizes, tiles, wanted, *refs):
    payload_refs, refs = refs[:n_payloads], refs[-(2 * len(wanted) + 10):]
    where = [(ref, index) for ref in payload_refs for index in range(ref.shape[0] // stride)]
    list_refs, row_ref, tables = refs[:len(wanted)], refs[len(wanted)], refs[len(wanted) + 1:-len(wanted) - 2]
    drafts, arrived, summed = refs[-len(wanted) - 2:-2], refs[-2], refs[-1]
    copies = [
        pltpu.make_async_copy(draft, ref, arrived.at[place])
        for place, (draft, ref) in enumerate(zip(drafts, list_refs))]
    capacity, depth, frames = sizes
    width = span * capacity
    extent = row_ref.shape[1]
    ray_tiles = row_ref.shape[0] // span
    height = -(-(7 * depth + 2) // 16) * 16
    lanes = drafts[0].shape[1]
    me = lax.axis_index("slab").astype(I32)
    parity = lax.rem(me, span)
    first_slot = (me - parity) * capacity
    part = 0 if n_payloads > 1 else lax.div(first_slot, extent)
    shift = lax.rem(extent - lax.rem(first_slot, extent), extent)

    def collect(member, lined, payload_ref, within):
        at = within * stride + tiles * frames + part * height
        raw = payload_ref[pl.ds(pl.multiple_of(at, 16), height), :].astype(F32)
        offset = (raw[0:depth] + raw[depth:2 * depth]) + raw[2 * depth:3 * depth]
        slope = (raw[3 * depth:4 * depth] + raw[4 * depth:5 * depth]) + raw[5 * depth:6 * depth]
        fields = jnp.concatenate(
            [offset, slope, raw[6 * depth:7 * depth + 2],
             jnp.zeros((16 - 3 * depth - 2, extent), F32)], axis=0)
        fields = pltpu.roll(fields, shift, axis=1)
        lane = lax.broadcasted_iota(I32, fields.shape, 1)
        fields = jnp.where(lane < width, fields, 0.0)
        if lanes > extent:
            fields = jnp.concatenate(
                [fields, jnp.zeros((fields.shape[0], lanes - extent), F32)], axis=1)
        return lined + pltpu.roll(fields, member * width, axis=1)

    lined = jnp.zeros((16, lanes), F32)
    if members <= 16:
        for member in range(members):
            lined = collect(member, lined, *where[member])
    else:
        lined = lax.fori_loop(
            0, members, lambda member, lined: collect(member, lined, payload_refs[0], member), lined)

    slot = lax.broadcasted_iota(I32, (1, lanes), 1)
    within = lax.rem(slot, width)
    target = lax.bitwise_xor(lax.div(within, capacity), parity)
    ray = lined[3 * depth:3 * depth + 1]
    count = lined[3 * depth + 1:3 * depth + 2]
    alive = jnp.logical_and(lax.rem(within, capacity).astype(F32) < count, slot < members * width)

    table = jnp.concatenate(
        [slot.astype(F32), ray, target.astype(F32), lined[2 * depth:3 * depth],
         jnp.zeros((5 - depth, lanes), F32)], axis=0)
    order = lax.broadcasted_iota(I32, (lanes, lanes), 0)
    earlier = (lax.broadcasted_iota(I32, (lanes, lanes), 1) < order).astype(F32)
    for ref, kind, copy in zip(drafts, wanted, copies):
        taken = alive if kind is None else jnp.logical_and(alive, target == kind)
        taken = taken.astype(F32)
        position = contract_lanes(jnp.broadcast_to(taken, (8, lanes)), earlier)[0:1]
        position = jnp.where(taken > 0.0, position, -1.0).astype(I32)
        choose = jnp.broadcast_to(position, (lanes, lanes)) == order
        packed = (contract_lanes(table, choose.astype(F32)) + 0.5).astype(I32)
        total = jnp.sum(taken, axis=1, keepdims=True).astype(I32)
        line = jnp.where(slot < total, packed[0:1], lanes)
        base = packed[1:2] if kind is not None else packed[1:2] + packed[2:3] * ray_tiles
        member = lax.div(packed[0:1], width) * tiles
        rows = [line, base * frames]
        rows += [(packed[3 + level:4 + level] + member) * frames for level in range(depth)]
        rows += [jnp.zeros((5 - depth, lanes), I32), jnp.broadcast_to(total, (1, lanes))]
        ref[...] = jnp.concatenate(rows, axis=0)
        copy.start()

    columns = lined.T
    step = 32
    for row in range(0, lanes, step):
        total = None
        for level in range(depth):
            offset = columns[row:row + step, level:level + 1]
            slope = columns[row:row + step, depth + level:depth + level + 1]
            middle, weights = row_taps(offset, slope, extent)
            first, pair = column_taps(offset, slope, extent)
            wide = [weight.astype(F32) for weight in weights]
            values = [middle] + wide + [first] + [weight.astype(F32) for weight in pair]
            at = level * (lanes + 8) + row
            for ref, value in zip(tables, values):
                ref[at:at + step, :] = value
            parts = (wide[0] + wide[1]) + wide[2]
            total = parts if total is None else total + parts
        summed[row:row + step, :] = total
    for ref in tables:
        blank = jnp.ones if ref.dtype == I32 else jnp.zeros
        for level in range(depth):
            at = level * (lanes + 8) + lanes
            ref[at:at + 8, :] = blank((8, extent), ref.dtype)

    tile = lax.broadcasted_iota(I32, (span * ray_tiles, lanes), 0).astype(F32)
    place = ray + (target * ray_tiles).astype(F32)
    place = jnp.where(alive, place, -1.0)
    hot = (jnp.broadcast_to(place, tile.shape) == tile).astype(F32)
    row_ref[...] = jnp.dot(hot, summed[...], precision=HIGHEST, preferred_element_type=F32)
    for copy in copies:
        copy.wait()


def column_kernel(sizes, offset_ref, slope_ref, voxel_ref, live_ref, out_ref):
    capacity, depth, frames = sizes
    tiles = out_ref.shape[0] // frames
    slots = offset_ref.shape[1]
    extent = out_ref.shape[1]
    offsets = offset_ref[...].T
    slopes = slope_ref[...].T
    within = lax.rem(lax.broadcasted_iota(I32, (1, slots), 1), capacity).astype(F32)
    alive = jnp.broadcast_to(within, (tiles, slots)) < per_slot(live_ref, slots, capacity)
    total = jnp.zeros((tiles, extent), F32)
    for level in range(depth):
        unused, pair = column_taps(
            offsets[:, level:level + 1], slopes[:, level:level + 1], extent)
        tile_of = jnp.broadcast_to(voxel_ref[level:level + 1, :], (tiles, slots))
        match = tile_of == lax.broadcasted_iota(I32, (tiles, slots), 0)
        hot = jnp.logical_and(match, alive).astype(F32).astype(BF16)
        for weight in pair:
            total += jnp.dot(hot, weight, preferred_element_type=F32)
    out_ref[...] = repeat_rows(1.0 / jnp.maximum(total, 1.0), frames)


def pick(values, index):
    numbers = lax.GatherDimensionNumbers(
        offset_dims=(), collapsed_slice_dims=(1,), start_index_map=(1,),
        operand_batching_dims=(0,), start_indices_batching_dims=(0,))
    return lax.gather(
        values, index[:, :, None], numbers, slice_sizes=(1, 1),
        mode=lax.GatherScatterMode.PROMISE_IN_BOUNDS)


def pack_pair(first, second):
    kind = jnp.int16 if first.dtype == I32 else BF16
    return jnp.concatenate([first, second], axis=0).astype(kind)


def spread(ref, row, frames):
    return ref[pl.ds(row, frames, stride=0), :]


def tile_at(start, frames):
    return pl.ds(pl.multiple_of(start, frames), frames)


def for_slots(slots, body):
    def some(step, carry):
        for place in range(CHUNK):
            body(step * CHUNK + place, place)
        return carry

    lax.fori_loop(0, lax.div(slots[7, 0] + (CHUNK - 1), CHUNK), some, 0)


def for_rows(rows, body):
    step = 128
    if rows <= 8 * step:
        for start in range(0, rows, step):
            body(pl.ds(start, step))
        return

    def some(number, carry):
        body(pl.ds(pl.multiple_of(number * step, step), step))
        return carry

    lax.fori_loop(0, rows // step, some, 0)


def forward_kernel(sizes, n_values, members, start_row, n_sums, slots, *refs):
    capacity, depth, frames = sizes
    value_refs, tables, refs = refs[:n_values], refs[n_values:n_values + 4], refs[n_values + 4:]
    start_ref = None
    if start_row is not None:
        start_ref, refs = refs[0], refs[1:]
    sum_refs, (out_ref, wide, second) = refs[:n_sums], refs[n_sums:]
    rows = wide.shape[0] // members
    stride = sum(ref.shape[0] for ref in value_refs) // members
    rays = second.shape[0]
    line_step = tables[0].shape[0] // depth

    base = 0
    for ref in value_refs:
        def widen(member, carry, ref=ref, base=base):
            at = (base + member) * rows
            start = member * stride
            if not isinstance(member, int):
                at, start = pl.multiple_of(at, rows), pl.multiple_of(start, 16)
            wide[pl.ds(at, rows), :] = ref[pl.ds(start, rows), :].astype(F32)
            return carry

        here = ref.shape[0] // stride
        if here <= 8:
            for member in range(here):
                widen(member, 0)
        else:
            lax.fori_loop(0, here, widen, 0)
        base += here
    second[...] = jnp.zeros_like(second)
    if start_ref is None:
        out_ref[...] = jnp.zeros_like(out_ref)
    else:
        out_ref[0:rays, :] = start_ref[start_row:start_row + rays, :]
    if n_sums:
        half = sum_refs[0].shape[0] // 2
        out_ref[rays:, :] = sum([ref[half:, :] for ref in sum_refs[1:]], sum_refs[0][half:, :])

    def one(slot, place):
        line = slots[0, slot]
        taps = []
        for start in range(0, depth, 2):
            levels = range(start, start + 2)
            values = [wide[tile_at(slots[2 + level, slot], frames), :] for level in levels]
            middles = [spread(tables[0], line + level * line_step, frames) for level in levels]
            lower = [
                pick(pack_pair(value, value), pack_pair(middle - 1, middle)).astype(F32)
                for value, middle in zip(values, middles)]
            upper = pick(
                pack_pair(*values), pack_pair(*[middle + 1 for middle in middles])).astype(F32)
            for which, pair in enumerate(lower):
                taps.append((pair[0:frames], pair[frames:2 * frames],
                             upper[which * frames:(which + 1) * frames]))
        total = None
        for level, three in enumerate(taps):
            for ref, tap in zip(tables[1:], three):
                term = spread(ref, line + level * line_step, frames) * tap
                total = term if total is None else total + term
        projection = (out_ref, second)[place % 2]
        projection[tile_at(slots[1, slot], frames), :] += total.astype(BF16).astype(F32)

    for_slots(slots, one)
    out_ref[0:rays, :] += second[...]


def residual_kernel(frames, n_own, projection_ref, sinogram_ref, *refs):
    own, refs, out_ref = refs[:n_own], refs[n_own:-1], refs[-1]
    rays = out_ref.shape[0]
    ray_tiles = rays // frames
    total = sum([ref[0:ray_tiles, :] for ref in own[1:]], own[0][0:ray_tiles, :])
    projection = projection_ref[...]
    if refs:
        projection = projection + refs[0][0:rays, :]
        total = total + refs[-1][rays:, :]
    weight = repeat_rows(1.0 / jnp.maximum(total, 1.0), frames)
    out_ref[...] = ((sinogram_ref[...].astype(F32) - projection) * weight).astype(BF16)


def backward_kernel(sizes, n_parts, has_start, split, slots, *refs):
    capacity, depth, frames = sizes
    part_refs, tables, refs = refs[:n_parts], refs[n_parts:n_parts + 3], refs[n_parts + 3:]
    start_ref = None
    if has_start:
        start_ref, refs = refs[0], refs[1:]
    outs = refs[:len(split)] if split else refs[:1]
    residual, banks = refs[len(outs)], refs[len(outs) + 1:]
    rays = part_refs[0].shape[0]
    line_step = tables[0].shape[0] // depth
    for place, ref in enumerate(part_refs):
        residual[place * rays:(place + 1) * rays, :] = ref[...].astype(F32)

    def clear(at):
        for place, bank in enumerate(banks):
            if place == 0 and has_start:
                bank[at, :] = start_ref[at, :]
            else:
                bank[at, :] = jnp.zeros((at.size, bank.shape[1]), F32)

    for_rows(banks[0].shape[0], clear)

    def one(slot, place):
        line = slots[0, slot]
        values = residual[tile_at(slots[1, slot], frames), :]
        twice = pack_pair(values, values)
        for level in range(depth):
            row = line + level * line_step
            first = spread(tables[0], row, frames)
            taps = pick(twice, pack_pair(first, first + 1)).astype(F32)
            term = (spread(tables[1], row, frames) * taps[0:frames]
                    + spread(tables[2], row, frames) * taps[frames:2 * frames])
            banks[level % len(banks)][tile_at(slots[2 + level, slot], frames), :] += term

    for_slots(slots, one)

    def total(at):
        return sum([bank[at, :] for bank in banks[1:]], banks[0][at, :])

    if split:
        for ref, members in zip(outs, split):
            rows = ref.shape[0] // len(members)
            for place, member in enumerate(members):
                ref[place * rows:(place + 1) * rows, :] = total(pl.ds(member * rows, rows)).astype(ref.dtype)
    else:
        def finish(at):
            outs[0][at, :] = total(at).astype(outs[0].dtype)

        for_rows(outs[0].shape[0], finish)


def join_kernel(*refs):
    out_ref, at = refs[-1], 0
    for ref in refs[:-1]:
        out_ref[at:at + ref.shape[0], :] = ref[...]
        at += ref.shape[0]


def combine_kernel(members, sum_ref, y_ref, *piece_refs):
    rows = piece_refs[0].shape[0]
    for place, (member, ref) in enumerate(zip(members, piece_refs)):
        mine = sum_ref[member * rows:(member + 1) * rows, :]
        ref[...] = (mine + y_ref[place * rows:(place + 1) * rows, :].astype(F32)).astype(ref.dtype)


def update_kernel(n_pieces, volume_ref, column_ref, *refs):
    back = refs[0][...]
    for ref in refs[1:n_pieces]:
        back = back + ref[...].astype(F32)
    volume = volume_ref[...] + column_ref[...] * back
    for ref in refs[n_pieces:]:
        ref[...] = volume.astype(ref.dtype)


def call(kernel, name, mib, in_specs, out_shape, *operands, scratch=()):
    one = not isinstance(out_shape, list)
    return pl.pallas_call(
        kernel,
        out_shape=out_shape,
        in_specs=in_specs,
        out_specs=VMEM if one else [
            SMEM if getattr(out, "memory_space", None) == pltpu.SMEM else VMEM for out in out_shape],
        scratch_shapes=list(scratch),
        compiler_params=pltpu.CompilerParams(vmem_limit_bytes=mib * 1024 * 1024),
        name=name,
        cost_estimate=pl.CostEstimate(flops=4 * 10**9, bytes_accessed=8 * 10**6, transcendentals=0),
    )(*operands)


def exchange(values, n_slab, distance, other_distance=None):
    far = (distance, distance if other_distance is None else other_distance)
    return lax.ppermute(
        values, "slab",
        [(device, device ^ far[device.bit_count() % 2]) for device in range(n_slab)])


def shards(sinogram, start_volume, slot_voxel, slot_ray, live_count, block_slope, block_offset):
    n_slab = lax.axis_size("slab")
    n_slots, depth = slot_voxel.shape
    capacity = n_slots // n_slab
    ray_tiles, frames, extent = sinogram.shape
    voxel_tiles = start_volume.shape[0]
    rows = voxel_tiles * frames
    sizes = (capacity, depth, frames)
    paired = n_slab == 16
    span = 2 if paired else 1
    n_bank = 2 if paired else 1
    shape = jax.ShapeDtypeStruct
    n_rays = ray_tiles * frames
    volume = start_volume.reshape(rows, extent)
    sino = sinogram.reshape(n_rays, extent)
    slots_by_depth = (block_offset.T, block_slope.T, slot_voxel.T)
    live = live_count.reshape(1, n_slab)
    height = -(-(7 * depth + 2) // 16) * 16 * (n_slots // extent)
    operands = (volume, *slots_by_depth, slot_ray.reshape(1, n_slots), live)
    partners = ((0, 0), (9, 3), (5, 9), (12, 10), (15, 15)) if paired else ()
    size = rows + height // (n_slots // extent if paired else 1)
    payloads = call(
        functools.partial(pack_kernel, capacity, partners), "pack", 16, [HBM] * 6,
        [shape((size, extent), BF16)] * max(1, len(partners)),
        *[pltpu.with_memory_space_constraint(operand, pltpu.HBM) for operand in operands],
        scratch=[pltpu.VMEM(operand.shape, operand.dtype) for operand in operands]
        + [pltpu.SemaphoreType.DMA((6,)), pltpu.VMEM((height, extent), BF16)])
    payload = payloads[0]

    def setup(payloads, members, wanted, after=None):
        lanes = -(-members * span * capacity // 128) * 128
        lines = depth * (lanes + 8)
        table = [shape((lines, extent), I32)] + [shape((lines, extent), F32)] * 3
        table += [shape((lines, extent), I32)] + [shape((lines, extent), F32)] * 2
        n = len(wanted)
        out = [pltpu.SMEM((8, lanes), I32)] * n + [shape((span * ray_tiles, extent), F32)] + table
        waits = [] if after is None else [after]
        found = call(
            functools.partial(setup_kernel, len(payloads), members,
                              sum(one.shape[0] for one in payloads) // members, span, sizes,
                              voxel_tiles, wanted),
            "setup", 24, [VMEM] * len(payloads) + [ANY] * len(waits), out, *payloads, *waits,
            scratch=[pltpu.VMEM((8, lanes), I32)] * n
            + [pltpu.SemaphoreType.DMA((n,)), pltpu.VMEM((lanes, extent), F32)])
        return found[:n], found[n], found[n + 1:n + 5], found[n + 5:]

    def forward(slots, values, members, table, n_out, start=None, start_row=None, sums=()):
        operands = [pltpu.with_memory_space_constraint(slots, pltpu.SMEM), *values, *table] + ([] if start is None else [start]) + list(sums)
        extra = ray_tiles if sums else 0
        return call(
            functools.partial(forward_kernel, sizes, len(values), members, start_row, len(sums)),
            "forward", 16 if paired else 32, [SMEM] + [VMEM] * (len(operands) - 1),
            shape((n_out + extra, extent), F32), *operands,
            scratch=[pltpu.VMEM((members * rows, extent), F32), pltpu.VMEM((n_out, extent), F32)])

    def residual_of(projection, row_sums, *sibling):
        operands = [projection, sino, *row_sums, *sibling]
        return call(
            functools.partial(residual_kernel, frames, len(row_sums)), "residual", 16,
            [VMEM] * len(operands), shape((n_rays, extent), BF16), *operands)

    def backward(slots, parts, members, table, kind, start=None, split=()):
        operands = [pltpu.with_memory_space_constraint(slots, pltpu.SMEM), *parts, *table] + ([] if start is None else [start])
        return call(
            functools.partial(backward_kernel, sizes, len(parts), start is not None, split),
            "backward", 16 if paired else 32, [SMEM] + [VMEM] * (len(operands) - 1),
            [shape((len(some) * rows, extent), each) for some, each in zip(split, kind)]
            if split else shape((members * rows, extent), kind), *operands,
            scratch=[pltpu.VMEM((len(parts) * n_rays, extent), F32)]
            + [pltpu.VMEM((members * rows, extent), F32)] * n_bank)

    def join(*parts):
        total = sum(part.shape[0] for part in parts)
        return call(join_kernel, "join", 16, [VMEM] * len(parts), shape((total, extent), BF16), *parts)

    def update(volume, pieces, last):
        out = [shape((rows, extent), F32)] + ([] if last else [shape((rows, extent), BF16)])
        return call(
            functools.partial(update_kernel, len(pieces)), "update", 16,
            [VMEM] * (2 + len(pieces)), out, volume, column_weight, *pieces)

    column_weight = call(
        functools.partial(column_kernel, sizes), "column_weight", 16, [VMEM] * 4,
        shape((rows, extent), F32), *slots_by_depth, live)

    for sweep in range(ITERS):
        last = sweep + 1 == ITERS
        if paired:
            place_1, place_2, place_3, across = [
                exchange(one, n_slab, *pair) for one, pair in zip(payloads[1:], partners[1:])]
            z_part = join(payload, place_1, place_2)
            y_part = exchange(z_part, n_slab, 3, 5)
            along_z, along_y = (z_part, place_3), (y_part, across)
            if sweep == 0:
                (z_list,), z_rows, z_forward, z_backward = setup(along_z, 4, (None,))
            both = forward(z_list, along_z, 4, z_forward, 2 * n_rays)
            if sweep == 0:
                (own_list, other_list), y_rows, y_forward, y_backward = setup(
                    along_y, 4, (0, 1), after=both)
            other = exchange(
                forward(other_list, along_y, 4, y_forward, n_rays, both, n_rays,
                        (z_rows, y_rows) if sweep == 0 else ()), n_slab, 1)
            if sweep == 0:
                first_other = other
            own = forward(own_list, along_y, 4, y_forward, n_rays, both, 0)
            residual = residual_of(own, (z_rows, y_rows), other, first_other)
            other_residual = exchange(residual, n_slab, 1)
            y_sum = backward(own_list, [residual], 4, y_backward, F32)
            far_sum, near_sum = backward(
                other_list, [other_residual], 4, y_backward, (BF16, BF16), y_sum, ((1, 3), (0, 2)))
            far_part, near_part = exchange(far_sum, n_slab, 3, 5), exchange(near_sum, n_slab, 3, 5)
            z_sum = backward(z_list, [residual, other_residual], 4, z_backward, F32)
            piece = shape((rows, extent), BF16)
            piece_1, piece_3 = call(
                functools.partial(combine_kernel, (1, 3)), "combine", 16, [VMEM] * 2,
                [piece, piece], z_sum, far_part)
            got = [exchange(piece_1, n_slab, 9, 3), exchange(piece_3, n_slab, 12, 10)]
            own_piece, piece_2 = call(
                functools.partial(combine_kernel, (0, 2)), "combine", 16, [VMEM] * 2,
                [shape((rows, extent), F32), piece], z_sum, near_part)
            pieces = [own_piece, exchange(piece_2, n_slab, 5, 9), *got]
        else:
            everyone = lax.all_gather(payload, "slab", axis=0, tiled=True)
            if sweep == 0:
                (slots,), row_sums, to_rays, to_voxels = setup((everyone,), n_slab, (None,))
            projection = forward(slots, (everyone,), n_slab, to_rays, n_rays)
            residual = residual_of(projection, (row_sums,))
            sums = backward(slots, [residual], n_slab, to_voxels, BF16)
            parts = lax.all_to_all(
                sums.reshape(n_slab, rows, extent), "slab", split_axis=0, concat_axis=0, tiled=True)
            pieces = [jnp.sum(parts.astype(F32), axis=0)]
        volume, *rounded = update(volume, pieces, last)
        if not last:
            payload = rounded[0]
            payloads = [payload] * (1 + len(partners))
    return volume.reshape(start_volume.shape)


def solution(mesh):
    in_specs = (
        P(("scan", "slab"), None, None),
        P(("scan", "slab"), None, None),
        P(("scan", "slab"), None),
        P(("scan", "slab")),
        P(("scan", "slab")),
        P(("scan", "slab"), None),
        P(("scan", "slab"), None),
    )
    out_specs = P(("scan", "slab"), None, None)
    return jax.shard_map(shards, mesh=mesh, in_specs=in_specs, out_specs=out_specs, check_vma=False)
```

profile of v0, /device:TPU:0, one launch (start us, length us, event | category | flops | bytes accessed | tf_op | source)
XLA Modules:
  0.0 60.4 jit_solution(9859213664435299203)
XLA Ops:
  0.0 1.0 %pack.1 = (bf16[160,128]{1,0:T(8,128)(2,1)S(1)}, bf16[160,128]{1,0:T(8,128)(2,1)S(1)}, bf16[160,128]{1,0:T(8,128)(2,1)S(1)}, bf16[160,128]{1,0:T(8,128)(2,1)S(1)}, bf16[160,128]{1,0:T(8,128)(2,1)S(1)}) custom-call(f32[128,128]{1,0:T(8,128)} %bitcast.8, f32[4,256]{1,0:T(4,128)} %bitcast.12, f32[4,256]{1,0:T(4,128)} %bitcast.14, s32[4,256]{1,0:T(4,128)} %bitcast.16, ...), custom_call_target="tpu_custom_call" | custom-call | flops 4000000000 | bytes 8000000 | tf_op jit(solution)/shard_map/pack/pallas_call | solution.py:432
  1.1 3.5 %collective-permute-start = (bf16[160,128]{1,0:T(8,128)(2,1)S(1)}, bf16[160,128]{1,0:T(8,128)(2,1)S(1)}, u32[]{:S(2)}, u32[]{:S(2)}) collective-permute-start(bf16[160,128]{1,0:T(8,128)(2,1)S(1)} %get-tuple-element.44), channel_id=1, source_target_pairs={{0,9},{1,2},{2,1},{3,10},{4,7},{5,12},{6,15},{7,4},{8,11},{9,0},{1... | collective-permute-start | bytes 122888 | tf_op jit(solution)/shard_map/ppermute | solution.py:447
  4.6 1.9 %collective-permute-start.1 = (bf16[160,128]{1,0:T(8,128)(2,1)S(1)}, bf16[160,128]{1,0:T(8,128)(2,1)S(1)}, u32[]{:S(2)}, u32[]{:S(2)}) collective-permute-start(bf16[160,128]{1,0:T(8,128)(2,1)S(1)} %get-tuple-element.45), channel_id=1, source_target_pairs={{0,5},{1,8},{2,11},{3,6},{4,13},{5,0},{6,3},{7,14},{8,1},{9,12},{1... | collective-permute-start | bytes 122888 | tf_op jit(solution)/shard_map/ppermute | solution.py:447
  6.5 3.9 %collective-permute-start.4 = (bf16[160,128]{1,0:T(8,128)(2,1)S(1)}, bf16[160,128]{1,0:T(8,128)(2,1)S(1)}, u32[]{:S(2)}, u32[]{:S(2)}) collective-permute-start(bf16[160,128]{1,0:T(8,128)(2,1)S(1)} %get-tuple-element.48), channel_id=1, source_target_pairs={{0,15},{1,14},{2,13},{3,12},{4,11},{5,10},{6,9},{7,8},{8,7},{9,6},... | collective-permute-start | bytes 122888 | tf_op jit(solution)/shard_map/ppermute | solution.py:447
  10.4 1.1 %collective-permute-start.3 = (bf16[480,128]{1,0:T(8,128)(2,1)S(1)}, bf16[480,128]{1,0:T(8,128)(2,1)S(1)}, u32[]{:S(2)}, u32[]{:S(2)}) collective-permute-start(bf16[480,128]{1,0:T(8,128)(2,1)S(1)} %join.2.refs_0_), channel_id=1, source_target_pairs={{0,3},{1,4},{2,7},{3,0},{4,1},{5,6},{6,5},{7,2},{8,13},{9,10},{10,... | collective-permute-start | bytes 368648 | tf_op jit(solution)/shard_map/ppermute | solution.py:447
  11.5 0.8 %collective-permute-done.2.refs_1_ = bf16[160,128]{1,0:T(8,128)(2,1)S(1)} collective-permute-done((bf16[160,128]{1,0:T(8,128)(2,1)S(1)}, bf16[160,128]{1,0:T(8,128)(2,1)S(1)}, u32[]{:S(2)}, u32[]{:S(2)}) %collective-permute-start.2) | collective-permute-done | bytes 40992 | tf_op jit(solution)/shard_map/ppermute | solution.py:447
  12.4 1.5 %setup.2 = (s32[8,128]{1,0:T(8,128)S(4)}, f32[64,128]{1,0:T(8,128)S(1)}, s32[544,128]{1,0:T(8,128)S(1)}, f32[544,128]{1,0:T(8,128)S(1)}, f32[544,128]{1,0:T(8,12...) custom-call(bf16[480,128]{1,0:T(8,128)(2,1)S(1)} %join.2.refs_0_, ...), custom_call_target="tpu_custom_call" | custom-call | flops 4000000000 | bytes 8000000 | tf_op jit(solution)/shard_map/setup/pallas_call | solution.py:432
  13.9 1.5 %forward.6.refs_2_.refs_6_ = f32[512,128]{1,0:T(8,128)S(1)} custom-call(s32[8,128]{1,0:T(8,128)S(4)} %get-tuple-element.47.slots, bf16[480,128]{1,0:T(8,128)(2,1)S(1)} %join.2.refs_0_, bf16[160,128]{1,0:T(8,128)(2,1)S(1)} %collective-permute-done.2.refs_1_, s32[544,128]{1,0:T(8,128)S(1)} %get-tuple-element.49.refs_2_, ...), custom_call_target="tpu_custom_call" | custom-call | flops 4000000000 | bytes 8000000 | tf_op jit(solution)/shard_map/forward/pallas_call | solution.py:432
  15.4 1.6 %setup.3 = (s32[8,128]{1,0:T(8,128)S(4)}, s32[8,128]{1,0:T(8,128)S(4)}, f32[64,128]{1,0:T(8,128)S(1)}, s32[544,128]{1,0:T(8,128)S(1)}, f32[544,128]{1,0:T(8,128)...) custom-call(bf16[480,128]{1,0:T(8,128)(2,1)S(1)} %collective-permute, ...), custom_call_target="tpu_custom_call" | custom-call | flops 4000000000 | bytes 8000000 | tf_op jit(solution)/shard_map/setup/pallas_call | solution.py:432
  17.0 0.7 %forward.8 = f32[288,128]{1,0:T(8,128)S(1)} custom-call(s32[8,128]{1,0:T(8,128)S(4)} %get-tuple-element.60.slots, bf16[480,128]{1,0:T(8,128)(2,1)S(1)} %collective-permute-done.3.refs_0_, bf16[160,128]{1,0:T(8,128)(2,1)S(1)} %collective-permute-done.4.refs_1_, s32[544,128]{1,0:T(8,128)S(1)} %get-tuple-element.54.refs_2_, ...), custom_call_target="tpu_custom_call" | custom-call | flops 4000000000 | bytes 8000000 | tf_op jit(solution)/shard_map/forward/pallas_call | solution.py:432
  17.7 0.8 %collective-permute-start.5 = (f32[288,128]{1,0:T(8,128)S(1)}, f32[288,128]{1,0:T(8,128)S(1)}, u32[]{:S(2)}, u32[]{:S(2)}) collective-permute-start(f32[288,128]{1,0:T(8,128)S(1)} %forward.8), channel_id=1, source_target_pairs={{0,1},{1,0},{2,3},{3,2},{4,5},{5,4},{6,7},{7,6},{8,9},{9,8},{10,11... | collective-permute-start | bytes 442376 | tf_op jit(solution)/shard_map/ppermute | solution.py:447
  18.5 0.7 %forward.7.projection_ref = f32[256,128]{1,0:T(8,128)S(1)} custom-call(s32[8,128]{1,0:T(8,128)S(4)} %get-tuple-element.53.slots, bf16[480,128]{1,0:T(8,128)(2,1)S(1)} %collective-permute-done.3.refs_0_, bf16[160,128]{1,0:T(8,128)(2,1)S(1)} %collective-permute-done.4.refs_1_, s32[544,128]{1,0:T(8,128)S(1)} %get-tuple-element.54.refs_2_, ...), custom_call_target="tpu_custom_call" | custom-call | flops 4000000000 | bytes 8000000 | tf_op jit(solution)/shard_map/forward/pallas_call | solution.py:432
  21.5 2.5 %collective-permute-start.9 = (bf16[256,128]{1,0:T(8,128)(2,1)S(1)}, bf16[256,128]{1,0:T(8,128)(2,1)S(1)}, u32[]{:S(2)}, u32[]{:S(2)}) collective-permute-start(bf16[256,128]{1,0:T(8,128)(2,1)S(1)} %get-tuple-element.70), channel_id=1, source_target_pairs={{0,3},{1,4},{2,7},{3,0},{4,1},{5,6},{6,5},{7,2},{8,13},{9,10},{10,... | collective-permute-start | bytes 196616 | tf_op jit(solution)/shard_map/ppermute | solution.py:447
  24.1 1.2 %backward.6.sum_ref = f32[512,128]{1,0:T(8,128)S(1)} custom-call(s32[8,128]{1,0:T(8,128)S(4)} %get-tuple-element.47.slots, bf16[256,128]{1,0:T(8,128)(2,1)S(1)} %residual.2.refs_0_, bf16[256,128]{1,0:T(8,128)(2,1)S(1)} %collective-permute-done.6.refs_1_.refs_0_, s32[544,128]{1,0:T(8,128)S(1)} %get-tuple-element.61.refs_2_, ...), custom_call_target="tpu_custom_call" | custom-call | flops 4000000000 | bytes 8000000 | tf_op jit(solution)/shard_map/backward/pallas_call | solution.py:432
  26.0 0.7 %collective-permute-start.10 = (bf16[128,128]{1,0:T(8,128)(2,1)S(1)}, bf16[128,128]{1,0:T(8,128)(2,1)S(1)}, u32[]{:S(2)}, u32[]{:S(2)}) collective-permute-start(bf16[128,128]{1,0:T(8,128)(2,1)S(1)} %get-tuple-element.71), channel_id=1, source_target_pairs={{0,9},{1,2},{2,1},{3,10},{4,7},{5,12},{6,15},{7,4},{8,11},{9,0},{1... | collective-permute-start | bytes 98312 | tf_op jit(solution)/shard_map/ppermute | solution.py:447
  26.7 3.1 %collective-permute-start.11 = (bf16[128,128]{1,0:T(8,128)(2,1)S(1)}, bf16[128,128]{1,0:T(8,128)(2,1)S(1)}, u32[]{:S(2)}, u32[]{:S(2)}) collective-permute-start(bf16[128,128]{1,0:T(8,128)(2,1)S(1)} %get-tuple-element.72), channel_id=1, source_target_pairs={{0,12},{1,11},{2,8},{3,15},{4,14},{5,9},{6,10},{7,13},{8,2},{9,5},... | collective-permute-start | bytes 98312 | tf_op jit(solution)/shard_map/ppermute | solution.py:447
  31.2 1.6 %collective-permute-done.11.refs_3_ = bf16[128,128]{1,0:T(8,128)(2,1)S(1)} collective-permute-done((bf16[128,128]{1,0:T(8,128)(2,1)S(1)}, bf16[128,128]{1,0:T(8,128)(2,1)S(1)}, u32[]{:S(2)}, u32[]{:S(2)}) %collective-permute-start.11) | collective-permute-done | bytes 32800 | tf_op jit(solution)/shard_map/ppermute | solution.py:447
  32.8 1.1 %collective-permute-done.8.refs_1_ = bf16[128,128]{1,0:T(8,128)(2,1)S(1)} collective-permute-done((bf16[128,128]{1,0:T(8,128)(2,1)S(1)}, bf16[128,128]{1,0:T(8,128)(2,1)S(1)}, u32[]{:S(2)}, u32[]{:S(2)}) %collective-permute-start.8) | collective-permute-done | bytes 32800 | tf_op jit(solution)/shard_map/ppermute | solution.py:447
  34.0 2.2 %collective-permute-start.13 = (bf16[128,128]{1,0:T(8,128)(2,1)S(1)}, bf16[128,128]{1,0:T(8,128)(2,1)S(1)}, u32[]{:S(2)}, u32[]{:S(2)}) collective-permute-start(bf16[128,128]{1,0:T(8,128)(2,1)S(1)} %get-tuple-element.74.refs_0_), channel_id=1, source_target_pairs={{0,5},{1,8},{2,11},{3,6},{4,13},{5,0},{6,3},{7,14},{8,1},{9,12},{1... | collective-permute-start | bytes 98312 | tf_op jit(solution)/shard_map/ppermute | solution.py:447
  36.2 1.9 %collective-permute-start.16 = (bf16[128,128]{1,0:T(8,128)(2,1)S(1)}, bf16[128,128]{1,0:T(8,128)(2,1)S(1)}, u32[]{:S(2)}, u32[]{:S(2)}) collective-permute-start(bf16[128,128]{1,0:T(8,128)(2,1)S(1)} %get-tuple-element.74.refs_0_), channel_id=1, source_target_pairs={{0,12},{1,11},{2,8},{3,15},{4,14},{5,9},{6,10},{7,13},{8,2},{9,5},... | collective-permute-start | bytes 98312 | tf_op jit(solution)/shard_map/ppermute | solution.py:447
  38.9 2.3 %collective-permute-start.14 = (bf16[384,128]{1,0:T(8,128)(2,1)S(1)}, bf16[384,128]{1,0:T(8,128)(2,1)S(1)}, u32[]{:S(2)}, u32[]{:S(2)}) collective-permute-start(bf16[384,128]{1,0:T(8,128)(2,1)S(1)} %join.3.refs_0_), channel_id=1, source_target_pairs={{0,3},{1,4},{2,7},{3,0},{4,1},{5,6},{6,5},{7,2},{8,13},{9,10},{10,... | collective-permute-start | bytes 294920 | tf_op jit(solution)/shard_map/ppermute | solution.py:447
  41.9 1.5 %forward.9.refs_6_ = f32[512,128]{1,0:T(8,128)S(1)} custom-call(s32[8,128]{1,0:T(8,128)S(4)} %get-tuple-element.47.slots, bf16[384,128]{1,0:T(8,128)(2,1)S(1)} %join.3.refs_0_, bf16[128,128]{1,0:T(8,128)(2,1)S(1)} %collective-permute-done.16.refs_1_, s32[544,128]{1,0:T(8,128)S(1)} %get-tuple-element.49.refs_2_, f32[544,128]{1,0:T(8,128)S(1)} %get-tuple-element.50.refs_3_, ...), custom_call_target="tpu_custom_call" | custom-call | flops 4000000000 | bytes 8000000 | tf_op jit(solution)/shard_map/forward/pallas_call | solution.py:432
  43.4 0.9 %collective-permute-done.15.refs_1_ = bf16[128,128]{1,0:T(8,128)(2,1)S(1)} collective-permute-done((bf16[128,128]{1,0:T(8,128)(2,1)S(1)}, bf16[128,128]{1,0:T(8,128)(2,1)S(1)}, u32[]{:S(2)}, u32[]{:S(2)}) %collective-permute-start.15) | collective-permute-done | bytes 32800 | tf_op jit(solution)/shard_map/ppermute | solution.py:447
  44.3 0.7 %forward.11 = f32[256,128]{1,0:T(8,128)S(1)} custom-call(s32[8,128]{1,0:T(8,128)S(4)} %get-tuple-element.60.slots, bf16[384,128]{1,0:T(8,128)(2,1)S(1)} %collective-permute-done.14.refs_0_, bf16[128,128]{1,0:T(8,128)(2,1)S(1)} %collective-permute-done.15.refs_1_, s32[544,128]{1,0:T(8,128)S(1)} %get-tuple-element.54.refs_2_, ...), custom_call_target="tpu_custom_call" | custom-call | flops 4000000000 | bytes 8000000 | tf_op jit(solution)/shard_map/forward/pallas_call | solution.py:432
  45.7 0.7 %forward.10.projection_ref = f32[256,128]{1,0:T(8,128)S(1)} custom-call(s32[8,128]{1,0:T(8,128)S(4)} %get-tuple-element.53.slots, bf16[384,128]{1,0:T(8,128)(2,1)S(1)} %collective-permute-done.14.refs_0_, bf16[128,128]{1,0:T(8,128)(2,1)S(1)} %collective-permute-done.15.refs_1_, s32[544,128]{1,0:T(8,128)S(1)} %get-tuple-element.54.refs_2_, ...), custom_call_target="tpu_custom_call" | custom-call | flops 4000000000 | bytes 8000000 | tf_op jit(solution)/shard_map/forward/pallas_call | solution.py:432
  48.6 1.8 %collective-permute-start.21 = (bf16[256,128]{1,0:T(8,128)(2,1)S(1)}, bf16[256,128]{1,0:T(8,128)(2,1)S(1)}, u32[]{:S(2)}, u32[]{:S(2)}) collective-permute-start(bf16[256,128]{1,0:T(8,128)(2,1)S(1)} %get-tuple-element.78), channel_id=1, source_target_pairs={{0,3},{1,4},{2,7},{3,0},{4,1},{5,6},{6,5},{7,2},{8,13},{9,10},{10,... | collective-permute-start | bytes 196616 | tf_op jit(solution)/shard_map/ppermute | solution.py:447
  50.5 1.2 %backward.9.sum_ref = f32[512,128]{1,0:T(8,128)S(1)} custom-call(s32[8,128]{1,0:T(8,128)S(4)} %get-tuple-element.47.slots, bf16[256,128]{1,0:T(8,128)(2,1)S(1)} %residual.3.refs_0_, bf16[256,128]{1,0:T(8,128)(2,1)S(1)} %collective-permute-done.18.refs_1_.refs_0_, s32[544,128]{1,0:T(8,128)S(1)} %get-tuple-element.61.refs_2_, ...), custom_call_target="tpu_custom_call" | custom-call | flops 4000000000 | bytes 8000000 | tf_op jit(solution)/shard_map/backward/pallas_call | solution.py:432
  51.6 0.7 %collective-permute-done.21.y_ref = bf16[256,128]{1,0:T(8,128)(2,1)S(1)} collective-permute-done((bf16[256,128]{1,0:T(8,128)(2,1)S(1)}, bf16[256,128]{1,0:T(8,128)(2,1)S(1)}, u32[]{:S(2)}, u32[]{:S(2)}) %collective-permute-start.21) | collective-permute-done | bytes 65568 | tf_op jit(solution)/shard_map/ppermute | solution.py:447
  52.4 1.4 %collective-permute-start.22 = (bf16[128,128]{1,0:T(8,128)(2,1)S(1)}, bf16[128,128]{1,0:T(8,128)(2,1)S(1)}, u32[]{:S(2)}, u32[]{:S(2)}) collective-permute-start(bf16[128,128]{1,0:T(8,128)(2,1)S(1)} %get-tuple-element.79), channel_id=1, source_target_pairs={{0,9},{1,2},{2,1},{3,10},{4,7},{5,12},{6,15},{7,4},{8,11},{9,0},{1... | collective-permute-start | bytes 98312 | tf_op jit(solution)/shard_map/ppermute | solution.py:447
  53.8 1.5 %collective-permute-start.23 = (bf16[128,128]{1,0:T(8,128)(2,1)S(1)}, bf16[128,128]{1,0:T(8,128)(2,1)S(1)}, u32[]{:S(2)}, u32[]{:S(2)}) collective-permute-start(bf16[128,128]{1,0:T(8,128)(2,1)S(1)} %get-tuple-element.80), channel_id=1, source_target_pairs={{0,12},{1,11},{2,8},{3,15},{4,14},{5,9},{6,10},{7,13},{8,2},{9,5},... | collective-permute-start | bytes 98312 | tf_op jit(solution)/shard_map/ppermute | solution.py:447
  55.5 1.2 %collective-permute-done.22.refs_2_ = bf16[128,128]{1,0:T(8,128)(2,1)S(1)} collective-permute-done((bf16[128,128]{1,0:T(8,128)(2,1)S(1)}, bf16[128,128]{1,0:T(8,128)(2,1)S(1)}, u32[]{:S(2)}, u32[]{:S(2)}) %collective-permute-start.22) | collective-permute-done | bytes 32800 | tf_op jit(solution)/shard_map/ppermute | solution.py:447
  56.7 3.0 %collective-permute-done.23.refs_3_ = bf16[128,128]{1,0:T(8,128)(2,1)S(1)} collective-permute-done((bf16[128,128]{1,0:T(8,128)(2,1)S(1)}, bf16[128,128]{1,0:T(8,128)(2,1)S(1)}, u32[]{:S(2)}, u32[]{:S(2)}) %collective-permute-start.23) | collective-permute-done | bytes 32800 | tf_op jit(solution)/shard_map/ppermute | solution.py:447
  (54 shorter events, 9.6 us)
Async XLA Ops:
  1.1 9.3 %collective-permute-start = (bf16[160,128]{1,0:T(8,128)(2,1)S(1)}, bf16[160,128]{1,0:T(8,128)(2,1)S(1)}, u32[]{:S(2)}, u32[]{:S(2)}) collective-permute-start(bf16[160,128]{1,0:T(8,128)(2,1)S(1)} %get-tuple-element.44), channel_id=1, source_target_pairs={{0,9},{1,2},{2,1},{3,10},{4,7},{5,12},{6,15},{7,4},{8,11},{9,0},{1... | collective-permute-start | bytes 122888 | tf_op jit(solution)/shard_map/ppermute | solution.py:447
  4.6 5.8 %collective-permute-start.1 = (bf16[160,128]{1,0:T(8,128)(2,1)S(1)}, bf16[160,128]{1,0:T(8,128)(2,1)S(1)}, u32[]{:S(2)}, u32[]{:S(2)}) collective-permute-start(bf16[160,128]{1,0:T(8,128)(2,1)S(1)} %get-tuple-element.45), channel_id=1, source_target_pairs={{0,5},{1,8},{2,11},{3,6},{4,13},{5,0},{6,3},{7,14},{8,1},{9,12},{1... | collective-permute-start | bytes 122888 | tf_op jit(solution)/shard_map/ppermute | solution.py:447
  6.5 5.9 %collective-permute-start.2 = (bf16[160,128]{1,0:T(8,128)(2,1)S(1)}, bf16[160,128]{1,0:T(8,128)(2,1)S(1)}, u32[]{:S(2)}, u32[]{:S(2)}) collective-permute-start(bf16[160,128]{1,0:T(8,128)(2,1)S(1)} %get-tuple-element.46), channel_id=1, source_target_pairs={{0,12},{1,11},{2,8},{3,15},{4,14},{5,9},{6,10},{7,13},{8,2},{9,5},... | collective-permute-start | bytes 122888 | tf_op jit(solution)/shard_map/ppermute | solution.py:447
  6.5 8.9 %collective-permute-start.4 = (bf16[160,128]{1,0:T(8,128)(2,1)S(1)}, bf16[160,128]{1,0:T(8,128)(2,1)S(1)}, u32[]{:S(2)}, u32[]{:S(2)}) collective-permute-start(bf16[160,128]{1,0:T(8,128)(2,1)S(1)} %get-tuple-element.48), channel_id=1, source_target_pairs={{0,15},{1,14},{2,13},{3,12},{4,11},{5,10},{6,9},{7,8},{8,7},{9,6},... | collective-permute-start | bytes 122888 | tf_op jit(solution)/shard_map/ppermute | solution.py:447
  10.4 4.9 %collective-permute-start.3 = (bf16[480,128]{1,0:T(8,128)(2,1)S(1)}, bf16[480,128]{1,0:T(8,128)(2,1)S(1)}, u32[]{:S(2)}, u32[]{:S(2)}) collective-permute-start(bf16[480,128]{1,0:T(8,128)(2,1)S(1)} %join.2.refs_0_), channel_id=1, source_target_pairs={{0,3},{1,4},{2,7},{3,0},{4,1},{5,6},{6,5},{7,2},{8,13},{9,10},{10,... | collective-permute-start | bytes 368648 | tf_op jit(solution)/shard_map/ppermute | solution.py:447
  17.7 1.8 %collective-permute-start.5 = (f32[288,128]{1,0:T(8,128)S(1)}, f32[288,128]{1,0:T(8,128)S(1)}, u32[]{:S(2)}, u32[]{:S(2)}) collective-permute-start(f32[288,128]{1,0:T(8,128)S(1)} %forward.8), channel_id=1, source_target_pairs={{0,1},{1,0},{2,3},{3,2},{4,5},{5,4},{6,7},{7,6},{8,9},{9,8},{10,11... | collective-permute-start | bytes 442376 | tf_op jit(solution)/shard_map/ppermute | solution.py:447
  18.5 1.0 %copy-start.1 = (bf16[32,8,128]{2,1,0:T(8,128)(2,1)S(1)}, bf16[32,8,128]{2,1,0:T(8,128)(2,1)}, u32[]{:S(2)}) copy-start(bf16[32,8,128]{2,1,0:T(8,128)(2,1)} %param.7) | copy-start | bytes 196612
  19.6 1.3 %collective-permute-start.6 = (bf16[256,128]{1,0:T(8,128)(2,1)S(1)}, bf16[256,128]{1,0:T(8,128)(2,1)S(1)}, u32[]{:S(2)}, u32[]{:S(2)}) collective-permute-start(bf16[256,128]{1,0:T(8,128)(2,1)S(1)} %residual.2.refs_0_), channel_id=1, source_target_pairs={{0,1},{1,0},{2,3},{3,2},{4,5},{5,4},{6,7},{7,6},{8,9},{9,8},{10,11... | collective-permute-start | bytes 196616 | tf_op jit(solution)/shard_map/ppermute | solution.py:447
  21.5 4.5 %collective-permute-start.9 = (bf16[256,128]{1,0:T(8,128)(2,1)S(1)}, bf16[256,128]{1,0:T(8,128)(2,1)S(1)}, u32[]{:S(2)}, u32[]{:S(2)}) collective-permute-start(bf16[256,128]{1,0:T(8,128)(2,1)S(1)} %get-tuple-element.70), channel_id=1, source_target_pairs={{0,3},{1,4},{2,7},{3,0},{4,1},{5,6},{6,5},{7,2},{8,13},{9,10},{10,... | collective-permute-start | bytes 196616 | tf_op jit(solution)/shard_map/ppermute | solution.py:447
  24.1 5.8 %collective-permute-start.7 = (bf16[256,128]{1,0:T(8,128)(2,1)S(1)}, bf16[256,128]{1,0:T(8,128)(2,1)S(1)}, u32[]{:S(2)}, u32[]{:S(2)}) collective-permute-start(bf16[256,128]{1,0:T(8,128)(2,1)S(1)} %get-tuple-element.67), channel_id=1, source_target_pairs={{0,3},{1,4},{2,7},{3,0},{4,1},{5,6},{6,5},{7,2},{8,13},{9,10},{10,... | collective-permute-start | bytes 196616 | tf_op jit(solution)/shard_map/ppermute | solution.py:447
  26.0 5.2 %collective-permute-start.10 = (bf16[128,128]{1,0:T(8,128)(2,1)S(1)}, bf16[128,128]{1,0:T(8,128)(2,1)S(1)}, u32[]{:S(2)}, u32[]{:S(2)}) collective-permute-start(bf16[128,128]{1,0:T(8,128)(2,1)S(1)} %get-tuple-element.71), channel_id=1, source_target_pairs={{0,9},{1,2},{2,1},{3,10},{4,7},{5,12},{6,15},{7,4},{8,11},{9,0},{1... | collective-permute-start | bytes 98312 | tf_op jit(solution)/shard_map/ppermute | solution.py:447
  26.7 3.3 %copy-start.2 = (f32[256,4]{0,1:T(4,128)S(1)}, f32[256,4]{0,1:T(4,128)}, u32[]{:S(2)}) copy-start(f32[256,4]{0,1:T(4,128)} %param.13) | copy-start | bytes 12292
  26.7 3.3 %copy-start.3 = (f32[256,4]{0,1:T(4,128)S(1)}, f32[256,4]{0,1:T(4,128)}, u32[]{:S(2)}) copy-start(f32[256,4]{0,1:T(4,128)} %param.12) | copy-start | bytes 12292
  26.7 3.3 %copy-start.4 = (s32[256,4]{0,1:T(4,128)S(1)}, s32[256,4]{0,1:T(4,128)}, u32[]{:S(2)}) copy-start(s32[256,4]{0,1:T(4,128)} %param.9) | copy-start | bytes 12292
  26.7 6.0 %collective-permute-start.11 = (bf16[128,128]{1,0:T(8,128)(2,1)S(1)}, bf16[128,128]{1,0:T(8,128)(2,1)S(1)}, u32[]{:S(2)}, u32[]{:S(2)}) collective-permute-start(bf16[128,128]{1,0:T(8,128)(2,1)S(1)} %get-tuple-element.72), channel_id=1, source_target_pairs={{0,12},{1,11},{2,8},{3,15},{4,14},{5,9},{6,10},{7,13},{8,2},{9,5},... | collective-permute-start | bytes 98312 | tf_op jit(solution)/shard_map/ppermute | solution.py:447
  29.9 0.7 %copy-start.5 = (s32[16]{0:T(128)S(1)}, s32[16]{0:T(128)}, u32[]{:S(2)}) copy-start(s32[16]{0:T(128)} %param.11) | copy-start | bytes 196
  29.9 4.0 %copy-start = (f32[16,8,128]{2,1,0:T(8,128)S(1)}, f32[16,8,128]{2,1,0:T(8,128)}, u32[]{:S(2)}) copy-start(f32[16,8,128]{2,1,0:T(8,128)} %param.8) | copy-start | bytes 196612
  29.9 4.0 %collective-permute-start.8 = (bf16[128,128]{1,0:T(8,128)(2,1)S(1)}, bf16[128,128]{1,0:T(8,128)(2,1)S(1)}, u32[]{:S(2)}, u32[]{:S(2)}) collective-permute-start(bf16[128,128]{1,0:T(8,128)(2,1)S(1)} %get-tuple-element.69), channel_id=1, source_target_pairs={{0,5},{1,8},{2,11},{3,6},{4,13},{5,0},{6,3},{7,14},{8,1},{9,12},{1... | collective-permute-start | bytes 98312 | tf_op jit(solution)/shard_map/ppermute | solution.py:447
  33.9 5.0 %collective-permute-start.12 = (bf16[128,128]{1,0:T(8,128)(2,1)S(1)}, bf16[128,128]{1,0:T(8,128)(2,1)S(1)}, u32[]{:S(2)}, u32[]{:S(2)}) collective-permute-start(bf16[128,128]{1,0:T(8,128)(2,1)S(1)} %get-tuple-element.74.refs_0_), channel_id=1, source_target_pairs={{0,9},{1,2},{2,1},{3,10},{4,7},{5,12},{6,15},{7,4},{8,11},{9,0},{1... | collective-permute-start | bytes 98312 | tf_op jit(solution)/shard_map/ppermute | solution.py:447
  34.0 4.9 %collective-permute-start.13 = (bf16[128,128]{1,0:T(8,128)(2,1)S(1)}, bf16[128,128]{1,0:T(8,128)(2,1)S(1)}, u32[]{:S(2)}, u32[]{:S(2)}) collective-permute-start(bf16[128,128]{1,0:T(8,128)(2,1)S(1)} %get-tuple-element.74.refs_0_), channel_id=1, source_target_pairs={{0,5},{1,8},{2,11},{3,6},{4,13},{5,0},{6,3},{7,14},{8,1},{9,12},{1... | collective-permute-start | bytes 98312 | tf_op jit(solution)/shard_map/ppermute | solution.py:447
  36.2 5.7 %collective-permute-start.16 = (bf16[128,128]{1,0:T(8,128)(2,1)S(1)}, bf16[128,128]{1,0:T(8,128)(2,1)S(1)}, u32[]{:S(2)}, u32[]{:S(2)}) collective-permute-start(bf16[128,128]{1,0:T(8,128)(2,1)S(1)} %get-tuple-element.74.refs_0_), channel_id=1, source_target_pairs={{0,12},{1,11},{2,8},{3,15},{4,14},{5,9},{6,10},{7,13},{8,2},{9,5},... | collective-permute-start | bytes 98312 | tf_op jit(solution)/shard_map/ppermute | solution.py:447
  38.1 6.2 %collective-permute-start.15 = (bf16[128,128]{1,0:T(8,128)(2,1)S(1)}, bf16[128,128]{1,0:T(8,128)(2,1)S(1)}, u32[]{:S(2)}, u32[]{:S(2)}) collective-permute-start(bf16[128,128]{1,0:T(8,128)(2,1)S(1)} %get-tuple-element.74.refs_0_), channel_id=1, source_target_pairs={{0,15},{1,14},{2,13},{3,12},{4,11},{5,10},{6,9},{7,8},{8,7},{9,6},... | collective-permute-start | bytes 98312 | tf_op jit(solution)/shard_map/ppermute | solution.py:447
  38.9 5.4 %collective-permute-start.14 = (bf16[384,128]{1,0:T(8,128)(2,1)S(1)}, bf16[384,128]{1,0:T(8,128)(2,1)S(1)}, u32[]{:S(2)}, u32[]{:S(2)}) collective-permute-start(bf16[384,128]{1,0:T(8,128)(2,1)S(1)} %join.3.refs_0_), channel_id=1, source_target_pairs={{0,3},{1,4},{2,7},{3,0},{4,1},{5,6},{6,5},{7,2},{8,13},{9,10},{10,... | collective-permute-start | bytes 294920 | tf_op jit(solution)/shard_map/ppermute | solution.py:447
  45.1 1.6 %collective-permute-start.17 = (f32[256,128]{1,0:T(8,128)S(1)}, f32[256,128]{1,0:T(8,128)S(1)}, u32[]{:S(2)}, u32[]{:S(2)}) collective-permute-start(f32[256,128]{1,0:T(8,128)S(1)} %forward.11), channel_id=1, source_target_pairs={{0,1},{1,0},{2,3},{3,2},{4,5},{5,4},{6,7},{7,6},{8,9},{9,8},{10,11... | collective-permute-start | bytes 393224 | tf_op jit(solution)/shard_map/ppermute | solution.py:447
  46.7 1.3 %collective-permute-start.18 = (bf16[256,128]{1,0:T(8,128)(2,1)S(1)}, bf16[256,128]{1,0:T(8,128)(2,1)S(1)}, u32[]{:S(2)}, u32[]{:S(2)}) collective-permute-start(bf16[256,128]{1,0:T(8,128)(2,1)S(1)} %residual.3.refs_0_), channel_id=1, source_target_pairs={{0,1},{1,0},{2,3},{3,2},{4,5},{5,4},{6,7},{7,6},{8,9},{9,8},{10,11... | collective-permute-start | bytes 196616 | tf_op jit(solution)/shard_map/ppermute | solution.py:447
  48.6 3.8 %collective-permute-start.21 = (bf16[256,128]{1,0:T(8,128)(2,1)S(1)}, bf16[256,128]{1,0:T(8,128)(2,1)S(1)}, u32[]{:S(2)}, u32[]{:S(2)}) collective-permute-start(bf16[256,128]{1,0:T(8,128)(2,1)S(1)} %get-tuple-element.78), channel_id=1, source_target_pairs={{0,3},{1,4},{2,7},{3,0},{4,1},{5,6},{6,5},{7,2},{8,13},{9,10},{10,... | collective-permute-start | bytes 196616 | tf_op jit(solution)/shard_map/ppermute | solution.py:447
  50.4 4.9 %collective-permute-start.19 = (bf16[256,128]{1,0:T(8,128)(2,1)S(1)}, bf16[256,128]{1,0:T(8,128)(2,1)S(1)}, u32[]{:S(2)}, u32[]{:S(2)}) collective-permute-start(bf16[256,128]{1,0:T(8,128)(2,1)S(1)} %get-tuple-element.75), channel_id=1, source_target_pairs={{0,3},{1,4},{2,7},{3,0},{4,1},{5,6},{6,5},{7,2},{8,13},{9,10},{10,... | collective-permute-start | bytes 196616 | tf_op jit(solution)/shard_map/ppermute | solution.py:447
  52.4 4.3 %collective-permute-start.22 = (bf16[128,128]{1,0:T(8,128)(2,1)S(1)}, bf16[128,128]{1,0:T(8,128)(2,1)S(1)}, u32[]{:S(2)}, u32[]{:S(2)}) collective-permute-start(bf16[128,128]{1,0:T(8,128)(2,1)S(1)} %get-tuple-element.79), channel_id=1, source_target_pairs={{0,9},{1,2},{2,1},{3,10},{4,7},{5,12},{6,15},{7,4},{8,11},{9,0},{1... | collective-permute-start | bytes 98312 | tf_op jit(solution)/shard_map/ppermute | solution.py:447
  53.8 5.9 %collective-permute-start.23 = (bf16[128,128]{1,0:T(8,128)(2,1)S(1)}, bf16[128,128]{1,0:T(8,128)(2,1)S(1)}, u32[]{:S(2)}, u32[]{:S(2)}) collective-permute-start(bf16[128,128]{1,0:T(8,128)(2,1)S(1)} %get-tuple-element.80), channel_id=1, source_target_pairs={{0,12},{1,11},{2,8},{3,15},{4,14},{5,9},{6,10},{7,13},{8,2},{9,5},... | collective-permute-start | bytes 98312 | tf_op jit(solution)/shard_map/ppermute | solution.py:447
  55.3 4.4 %collective-permute-start.20 = (bf16[128,128]{1,0:T(8,128)(2,1)S(1)}, bf16[128,128]{1,0:T(8,128)(2,1)S(1)}, u32[]{:S(2)}, u32[]{:S(2)}) collective-permute-start(bf16[128,128]{1,0:T(8,128)(2,1)S(1)} %get-tuple-element.77), channel_id=1, source_target_pairs={{0,5},{1,8},{2,11},{3,6},{4,13},{5,0},{6,3},{7,14},{8,1},{9,12},{1... | collective-permute-start | bytes 98312 | tf_op jit(solution)/shard_map/ppermute | solution.py:447
where the time goes:
time: 60.3 us; the launch traced here: 60.4 us
  starting transfers between devices  31.2 us (52%)
  Pallas kernels  16.3 us (27%)
  waiting for transfers between devices  12.1 us (20%)
    ppermute x24, starting transfers between devices, exchange(): lax.ppermute(values, 'slab', [(device, device ^ far[device.bit_count() %...  31.2 us
    pallas_call x26, Pallas kernels, call(): pl.pallas_call(kernel, out_shape=out_shape, in_specs=in_specs, out_specs=...  16.3 us
    ppermute x24, waiting for transfers between devices, exchange(): lax.ppermute(values, 'slab', [(device, device ^ far[device.bit_count() %...  12.1 us
  transfers between devices with their start and end apart: 24, of which 14 were waited for; matrix products, arithmetic and copies ran while one was open for 0% of the time, Pallas kernels for 17%

commit v1 on v0

--- a/solution.py
+++ b/solution.py
@@ -468,7 +468,7 @@
     live = live_count.reshape(1, n_slab)
     height = -(-(7 * depth + 2) // 16) * 16 * (n_slots // extent)
     operands = (volume, *slots_by_depth, slot_ray.reshape(1, n_slots), live)
-    partners = ((0, 0), (9, 3), (5, 9), (12, 10), (15, 15)) if paired else ()
+    partners = ((0, 0), (12, 3), (5, 10), (9, 9), (10, 12)) if paired else ()
     size = rows + height // (n_slots // extent if paired else 1)
     payloads = call(
         functools.partial(pack_kernel, capacity, partners), "pack", 16, [HBM] * 6,
@@ -565,11 +565,11 @@
             piece_1, piece_3 = call(
                 functools.partial(combine_kernel, (1, 3)), "combine", 16, [VMEM] * 2,
                 [piece, piece], z_sum, far_part)
-            got = [exchange(piece_1, n_slab, 9, 3), exchange(piece_3, n_slab, 12, 10)]
+            got = [exchange(piece_1, n_slab, 12, 3), exchange(piece_3, n_slab, 9)]
             own_piece, piece_2 = call(
                 functools.partial(combine_kernel, (0, 2)), "combine", 16, [VMEM] * 2,
                 [shape((rows, extent), F32), piece], z_sum, near_part)
-            pieces = [own_piece, exchange(piece_2, n_slab, 5, 9), *got]
+            pieces = [own_piece, exchange(piece_2, n_slab, 5, 10), *got]
         else:
             everyone = lax.all_gather(payload, "slab", axis=0, tiled=True)
             if sweep == 0:

time: 60.3 us -> 61.6 us (1.022); the launches traced: 60.4 us -> 60.9 us
  Pallas kernels: 16.3 us -> 18.8 us
  waiting for transfers between devices: 12.1 us -> 11 us
    pallas_call x26, Pallas kernels: 16.3 us -> 18.8 us  [call(): pl.pallas_call(kernel, out_shape=out_shape, in_specs=in_specs, out_specs=...]
    ppermute x24, waiting for transfers between devices: 12.1 us -> 11 us  [exchange(): lax.ppermute(values, 'slab', [(device, device ^ far[device.bit_count() %...]
  transfers between devices with their start and end apart: 24 -> 24, of which waited for: 14 -> 15; matrix products, arithmetic and copies ran while one was open for 0% -> 0% of each run, Pallas kernels for 17% -> 19%
where the time goes in v1:
time: 61.6 us; the launch traced here: 60.9 us
  starting transfers between devices  30.6 us (50%)
  Pallas kernels  18.8 us (31%)
  waiting for transfers between devices  11 us (18%)
    ppermute x24, starting transfers between devices, exchange(): lax.ppermute(values, 'slab', [(device, device ^ far[device.bit_count() %...  30.6 us
    pallas_call x26, Pallas kernels, call(): pl.pallas_call(kernel, out_shape=out_shape, in_specs=in_specs, out_specs=...  18.8 us
    ppermute x24, waiting for transfers between devices, exchange(): lax.ppermute(values, 'slab', [(device, device ^ far[device.bit_count() %...  11 us
  transfers between devices with their start and end apart: 24, of which 15 were waited for; matrix products, arithmetic and copies ran while one was open for 0% of the time, Pallas kernels for 19%

profile of v1, /device:TPU:0, one launch (start us, length us, event | category | flops | bytes accessed | tf_op | source)
XLA Modules:
  0.0 60.9 jit_solution(9053248856092567873)
XLA Ops:
  0.0 1.0 %pack.1 = (bf16[160,128]{1,0:T(8,128)(2,1)S(1)}, bf16[160,128]{1,0:T(8,128)(2,1)S(1)}, bf16[160,128]{1,0:T(8,128)(2,1)S(1)}, bf16[160,128]{1,0:T(8,128)(2,1)S(1)}, bf16[160,128]{1,0:T(8,128)(2,1)S(1)}) custom-call(f32[128,128]{1,0:T(8,128)} %bitcast.8, f32[4,256]{1,0:T(4,128)} %bitcast.12, f32[4,256]{1,0:T(4,128)} %bitcast.14, s32[4,256]{1,0:T(4,128)} %bitcast.16, ...), custom_call_target="tpu_custom_call" | custom-call | flops 4000000000 | bytes 8000000 | tf_op jit(solution)/shard_map/pack/pallas_call | solution.py:432
  1.1 5.1 %collective-permute-start = (bf16[160,128]{1,0:T(8,128)(2,1)S(1)}, bf16[160,128]{1,0:T(8,128)(2,1)S(1)}, u32[]{:S(2)}, u32[]{:S(2)}) collective-permute-start(bf16[160,128]{1,0:T(8,128)(2,1)S(1)} %get-tuple-element.44), channel_id=1, source_target_pairs={{0,12},{1,2},{2,1},{3,15},{4,7},{5,9},{6,10},{7,4},{8,11},{9,5},{1... | collective-permute-start | bytes 122888 | tf_op jit(solution)/shard_map/ppermute | solution.py:447
  6.6 2.8 %collective-permute-start.4 = (bf16[160,128]{1,0:T(8,128)(2,1)S(1)}, bf16[160,128]{1,0:T(8,128)(2,1)S(1)}, u32[]{:S(2)}, u32[]{:S(2)}) collective-permute-start(bf16[160,128]{1,0:T(8,128)(2,1)S(1)} %get-tuple-element.48), channel_id=1, source_target_pairs={{0,10},{1,13},{2,14},{3,9},{4,8},{5,15},{6,12},{7,11},{8,4},{9,3},... | collective-permute-start | bytes 122888 | tf_op jit(solution)/shard_map/ppermute | solution.py:447
  9.6 0.7 %collective-permute-start.3 = (bf16[480,128]{1,0:T(8,128)(2,1)S(1)}, bf16[480,128]{1,0:T(8,128)(2,1)S(1)}, u32[]{:S(2)}, u32[]{:S(2)}) collective-permute-start(bf16[480,128]{1,0:T(8,128)(2,1)S(1)} %join.2.refs_0_), channel_id=1, source_target_pairs={{0,3},{1,4},{2,7},{3,0},{4,1},{5,6},{6,5},{7,2},{8,13},{9,10},{10,... | collective-permute-start | bytes 368648 | tf_op jit(solution)/shard_map/ppermute | solution.py:447
  10.5 1.5 %setup.2 = (s32[8,128]{1,0:T(8,128)S(4)}, f32[64,128]{1,0:T(8,128)S(1)}, s32[544,128]{1,0:T(8,128)S(1)}, f32[544,128]{1,0:T(8,128)S(1)}, f32[544,128]{1,0:T(8,12...) custom-call(bf16[480,128]{1,0:T(8,128)(2,1)S(1)} %join.2.refs_0_, ...), custom_call_target="tpu_custom_call" | custom-call | flops 4000000000 | bytes 8000000 | tf_op jit(solution)/shard_map/setup/pallas_call | solution.py:432
  12.0 1.8 %forward.6.refs_2_.refs_6_ = f32[512,128]{1,0:T(8,128)S(1)} custom-call(s32[8,128]{1,0:T(8,128)S(4)} %get-tuple-element.47.slots, bf16[480,128]{1,0:T(8,128)(2,1)S(1)} %join.2.refs_0_, bf16[160,128]{1,0:T(8,128)(2,1)S(1)} %collective-permute-done.2.refs_1_, s32[544,128]{1,0:T(8,128)S(1)} %get-tuple-element.49.refs_2_, ...), custom_call_target="tpu_custom_call" | custom-call | flops 4000000000 | bytes 8000000 | tf_op jit(solution)/shard_map/forward/pallas_call | solution.py:432
  14.4 1.6 %setup.3 = (s32[8,128]{1,0:T(8,128)S(4)}, s32[8,128]{1,0:T(8,128)S(4)}, f32[64,128]{1,0:T(8,128)S(1)}, s32[544,128]{1,0:T(8,128)S(1)}, f32[544,128]{1,0:T(8,128)...) custom-call(bf16[480,128]{1,0:T(8,128)(2,1)S(1)} %collective-permute, ...), custom_call_target="tpu_custom_call" | custom-call | flops 4000000000 | bytes 8000000 | tf_op jit(solution)/shard_map/setup/pallas_call | solution.py:432
  16.0 1.1 %forward.8 = f32[288,128]{1,0:T(8,128)S(1)} custom-call(s32[8,128]{1,0:T(8,128)S(4)} %get-tuple-element.60.slots, bf16[480,128]{1,0:T(8,128)(2,1)S(1)} %collective-permute-done.3.refs_0_, bf16[160,128]{1,0:T(8,128)(2,1)S(1)} %collective-permute-done.4.refs_1_, s32[544,128]{1,0:T(8,128)S(1)} %get-tuple-element.54.refs_2_, ...), custom_call_target="tpu_custom_call" | custom-call | flops 4000000000 | bytes 8000000 | tf_op jit(solution)/shard_map/forward/pallas_call | solution.py:432
  17.2 0.7 %forward.7.projection_ref = f32[256,128]{1,0:T(8,128)S(1)} custom-call(s32[8,128]{1,0:T(8,128)S(4)} %get-tuple-element.53.slots, bf16[480,128]{1,0:T(8,128)(2,1)S(1)} %collective-permute-done.3.refs_0_, bf16[160,128]{1,0:T(8,128)(2,1)S(1)} %collective-permute-done.4.refs_1_, s32[544,128]{1,0:T(8,128)S(1)} %get-tuple-element.54.refs_2_, ...), custom_call_target="tpu_custom_call" | custom-call | flops 4000000000 | bytes 8000000 | tf_op jit(solution)/shard_map/forward/pallas_call | solution.py:432
  19.9 0.9 %backward.8 = (bf16[256,128]{1,0:T(8,128)(2,1)S(1)}, bf16[256,128]{1,0:T(8,128)(2,1)S(1)}) custom-call(s32[8,128]{1,0:T(8,128)S(4)} %get-tuple-element.60.slots, bf16[256,128]{1,0:T(8,128)(2,1)S(1)} %collective-permute-done.6.refs_1_.refs_0_, s32[544,128]{1,0:T(8,128)S(1)} %get-tuple-element.64.refs_1_, f32[544,128]{1,0:T(8,128)S(1)} %get-tuple-element.65.refs_2_, ...), custom_call_target="tpu_custom_call" | custom-call | flops 4000000000 | bytes 8000000 | tf_op jit(solution)/shard_map/backward/pallas_call | solution.py:432
  20.8 0.9 %collective-permute-start.9 = (bf16[256,128]{1,0:T(8,128)(2,1)S(1)}, bf16[256,128]{1,0:T(8,128)(2,1)S(1)}, u32[]{:S(2)}, u32[]{:S(2)}) collective-permute-start(bf16[256,128]{1,0:T(8,128)(2,1)S(1)} %get-tuple-element.70), channel_id=1, source_target_pairs={{0,3},{1,4},{2,7},{3,0},{4,1},{5,6},{6,5},{7,2},{8,13},{9,10},{10,... | collective-permute-start | bytes 196616 | tf_op jit(solution)/shard_map/ppermute | solution.py:447
  21.7 1.0 %collective-permute-start.7 = (bf16[256,128]{1,0:T(8,128)(2,1)S(1)}, bf16[256,128]{1,0:T(8,128)(2,1)S(1)}, u32[]{:S(2)}, u32[]{:S(2)}) collective-permute-start(bf16[256,128]{1,0:T(8,128)(2,1)S(1)} %get-tuple-element.67), channel_id=1, source_target_pairs={{0,3},{1,4},{2,7},{3,0},{4,1},{5,6},{6,5},{7,2},{8,13},{9,10},{10,... | collective-permute-start | bytes 196616 | tf_op jit(solution)/shard_map/ppermute | solution.py:447
  22.6 1.5 %backward.6.sum_ref = f32[512,128]{1,0:T(8,128)S(1)} custom-call(s32[8,128]{1,0:T(8,128)S(4)} %get-tuple-element.47.slots, bf16[256,128]{1,0:T(8,128)(2,1)S(1)} %residual.2.refs_0_, bf16[256,128]{1,0:T(8,128)(2,1)S(1)} %collective-permute-done.6.refs_1_.refs_0_, s32[544,128]{1,0:T(8,128)S(1)} %get-tuple-element.61.refs_2_, ...), custom_call_target="tpu_custom_call" | custom-call | flops 4000000000 | bytes 8000000 | tf_op jit(solution)/shard_map/backward/pallas_call | solution.py:432
  24.6 4.2 %collective-permute-start.10 = (bf16[128,128]{1,0:T(8,128)(2,1)S(1)}, bf16[128,128]{1,0:T(8,128)(2,1)S(1)}, u32[]{:S(2)}, u32[]{:S(2)}) collective-permute-start(bf16[128,128]{1,0:T(8,128)(2,1)S(1)} %get-tuple-element.71), channel_id=1, source_target_pairs={{0,12},{1,2},{2,1},{3,15},{4,7},{5,9},{6,10},{7,4},{8,11},{9,5},{1... | collective-permute-start | bytes 98312 | tf_op jit(solution)/shard_map/ppermute | solution.py:447
  30.7 2.3 %collective-permute-done.11.refs_3_ = bf16[128,128]{1,0:T(8,128)(2,1)S(1)} collective-permute-done((bf16[128,128]{1,0:T(8,128)(2,1)S(1)}, bf16[128,128]{1,0:T(8,128)(2,1)S(1)}, u32[]{:S(2)}, u32[]{:S(2)}) %collective-permute-start.11) | collective-permute-done | bytes 32800 | tf_op jit(solution)/shard_map/ppermute | solution.py:447
  33.1 2.0 %collective-permute-start.12 = (bf16[128,128]{1,0:T(8,128)(2,1)S(1)}, bf16[128,128]{1,0:T(8,128)(2,1)S(1)}, u32[]{:S(2)}, u32[]{:S(2)}) collective-permute-start(bf16[128,128]{1,0:T(8,128)(2,1)S(1)} %get-tuple-element.74.refs_0_), channel_id=1, source_target_pairs={{0,12},{1,2},{2,1},{3,15},{4,7},{5,9},{6,10},{7,4},{8,11},{9,5},{1... | collective-permute-start | bytes 98312 | tf_op jit(solution)/shard_map/ppermute | solution.py:447
  35.3 2.0 %collective-permute-start.16 = (bf16[128,128]{1,0:T(8,128)(2,1)S(1)}, bf16[128,128]{1,0:T(8,128)(2,1)S(1)}, u32[]{:S(2)}, u32[]{:S(2)}) collective-permute-start(bf16[128,128]{1,0:T(8,128)(2,1)S(1)} %get-tuple-element.74.refs_0_), channel_id=1, source_target_pairs={{0,9},{1,8},{2,11},{3,10},{4,13},{5,12},{6,15},{7,14},{8,1},{9,0},... | collective-permute-start | bytes 98312 | tf_op jit(solution)/shard_map/ppermute | solution.py:447
  37.3 2.0 %collective-permute-start.15 = (bf16[128,128]{1,0:T(8,128)(2,1)S(1)}, bf16[128,128]{1,0:T(8,128)(2,1)S(1)}, u32[]{:S(2)}, u32[]{:S(2)}) collective-permute-start(bf16[128,128]{1,0:T(8,128)(2,1)S(1)} %get-tuple-element.74.refs_0_), channel_id=1, source_target_pairs={{0,10},{1,13},{2,14},{3,9},{4,8},{5,15},{6,12},{7,11},{8,4},{9,3},... | collective-permute-start | bytes 98312 | tf_op jit(solution)/shard_map/ppermute | solution.py:447
  39.3 1.2 %collective-permute-start.14 = (bf16[384,128]{1,0:T(8,128)(2,1)S(1)}, bf16[384,128]{1,0:T(8,128)(2,1)S(1)}, u32[]{:S(2)}, u32[]{:S(2)}) collective-permute-start(bf16[384,128]{1,0:T(8,128)(2,1)S(1)} %join.3.refs_0_), channel_id=1, source_target_pairs={{0,3},{1,4},{2,7},{3,0},{4,1},{5,6},{6,5},{7,2},{8,13},{9,10},{10,... | collective-permute-start | bytes 294920 | tf_op jit(solution)/shard_map/ppermute | solution.py:447
  40.5 1.8 %forward.9.refs_6_ = f32[512,128]{1,0:T(8,128)S(1)} custom-call(s32[8,128]{1,0:T(8,128)S(4)} %get-tuple-element.47.slots, bf16[384,128]{1,0:T(8,128)(2,1)S(1)} %join.3.refs_0_, bf16[128,128]{1,0:T(8,128)(2,1)S(1)} %collective-permute-done.16.refs_1_, s32[544,128]{1,0:T(8,128)S(1)} %get-tuple-element.49.refs_2_, f32[544,128]{1,0:T(8,128)S(1)} %get-tuple-element.50.refs_3_, ...), custom_call_target="tpu_custom_call" | custom-call | flops 4000000000 | bytes 8000000 | tf_op jit(solution)/shard_map/forward/pallas_call | solution.py:432
  42.3 1.3 %collective-permute-done.15.refs_1_ = bf16[128,128]{1,0:T(8,128)(2,1)S(1)} collective-permute-done((bf16[128,128]{1,0:T(8,128)(2,1)S(1)}, bf16[128,128]{1,0:T(8,128)(2,1)S(1)}, u32[]{:S(2)}, u32[]{:S(2)}) %collective-permute-start.15) | collective-permute-done | bytes 32800 | tf_op jit(solution)/shard_map/ppermute | solution.py:447
  43.7 1.1 %forward.11 = f32[256,128]{1,0:T(8,128)S(1)} custom-call(s32[8,128]{1,0:T(8,128)S(4)} %get-tuple-element.60.slots, bf16[384,128]{1,0:T(8,128)(2,1)S(1)} %collective-permute-done.14.refs_0_, bf16[128,128]{1,0:T(8,128)(2,1)S(1)} %collective-permute-done.15.refs_1_, s32[544,128]{1,0:T(8,128)S(1)} %get-tuple-element.54.refs_2_, ...), custom_call_target="tpu_custom_call" | custom-call | flops 4000000000 | bytes 8000000 | tf_op jit(solution)/shard_map/forward/pallas_call | solution.py:432
  44.8 1.1 %collective-permute-start.17 = (f32[256,128]{1,0:T(8,128)S(1)}, f32[256,128]{1,0:T(8,128)S(1)}, u32[]{:S(2)}, u32[]{:S(2)}) collective-permute-start(f32[256,128]{1,0:T(8,128)S(1)} %forward.11), channel_id=1, source_target_pairs={{0,1},{1,0},{2,3},{3,2},{4,5},{5,4},{6,7},{7,6},{8,9},{9,8},{10,11... | collective-permute-start | bytes 393224 | tf_op jit(solution)/shard_map/ppermute | solution.py:447
  45.9 0.7 %forward.10.projection_ref = f32[256,128]{1,0:T(8,128)S(1)} custom-call(s32[8,128]{1,0:T(8,128)S(4)} %get-tuple-element.53.slots, bf16[384,128]{1,0:T(8,128)(2,1)S(1)} %collective-permute-done.14.refs_0_, bf16[128,128]{1,0:T(8,128)(2,1)S(1)} %collective-permute-done.15.refs_1_, s32[544,128]{1,0:T(8,128)S(1)} %get-tuple-element.54.refs_2_, ...), custom_call_target="tpu_custom_call" | custom-call | flops 4000000000 | bytes 8000000 | tf_op jit(solution)/shard_map/forward/pallas_call | solution.py:432
  48.2 0.9 %backward.11 = (bf16[256,128]{1,0:T(8,128)(2,1)S(1)}, bf16[256,128]{1,0:T(8,128)(2,1)S(1)}) custom-call(s32[8,128]{1,0:T(8,128)S(4)} %get-tuple-element.60.slots, bf16[256,128]{1,0:T(8,128)(2,1)S(1)} %collective-permute-done.18.refs_1_.refs_0_, s32[544,128]{1,0:T(8,128)S(1)} %get-tuple-element.64.refs_1_, f32[544,128]{1,0:T(8,128)S(1)} %get-tuple-element.65.refs_2_, ...), custom_call_target="tpu_custom_call" | custom-call | flops 4000000000 | bytes 8000000 | tf_op jit(solution)/shard_map/backward/pallas_call | solution.py:432
  49.7 1.2 %collective-permute-start.19 = (bf16[256,128]{1,0:T(8,128)(2,1)S(1)}, bf16[256,128]{1,0:T(8,128)(2,1)S(1)}, u32[]{:S(2)}, u32[]{:S(2)}) collective-permute-start(bf16[256,128]{1,0:T(8,128)(2,1)S(1)} %get-tuple-element.75), channel_id=1, source_target_pairs={{0,3},{1,4},{2,7},{3,0},{4,1},{5,6},{6,5},{7,2},{8,13},{9,10},{10,... | collective-permute-start | bytes 196616 | tf_op jit(solution)/shard_map/ppermute | solution.py:447
  50.9 1.5 %backward.9.sum_ref = f32[512,128]{1,0:T(8,128)S(1)} custom-call(s32[8,128]{1,0:T(8,128)S(4)} %get-tuple-element.47.slots, bf16[256,128]{1,0:T(8,128)(2,1)S(1)} %residual.3.refs_0_, bf16[256,128]{1,0:T(8,128)(2,1)S(1)} %collective-permute-done.18.refs_1_.refs_0_, s32[544,128]{1,0:T(8,128)S(1)} %get-tuple-element.61.refs_2_, ...), custom_call_target="tpu_custom_call" | custom-call | flops 4000000000 | bytes 8000000 | tf_op jit(solution)/shard_map/backward/pallas_call | solution.py:432
  52.9 2.3 %collective-permute-start.22 = (bf16[128,128]{1,0:T(8,128)(2,1)S(1)}, bf16[128,128]{1,0:T(8,128)(2,1)S(1)}, u32[]{:S(2)}, u32[]{:S(2)}) collective-permute-start(bf16[128,128]{1,0:T(8,128)(2,1)S(1)} %get-tuple-element.79), channel_id=1, source_target_pairs={{0,12},{1,2},{2,1},{3,15},{4,7},{5,9},{6,10},{7,4},{8,11},{9,5},{1... | collective-permute-start | bytes 98312 | tf_op jit(solution)/shard_map/ppermute | solution.py:447
  55.2 1.5 %collective-permute-start.23 = (bf16[128,128]{1,0:T(8,128)(2,1)S(1)}, bf16[128,128]{1,0:T(8,128)(2,1)S(1)}, u32[]{:S(2)}, u32[]{:S(2)}) collective-permute-start(bf16[128,128]{1,0:T(8,128)(2,1)S(1)} %get-tuple-element.80), channel_id=1, source_target_pairs={{0,9},{1,8},{2,11},{3,10},{4,13},{5,12},{6,15},{7,14},{8,1},{9,0},... | collective-permute-start | bytes 98312 | tf_op jit(solution)/shard_map/ppermute | solution.py:447
  57.2 1.5 %collective-permute-done.22.refs_2_ = bf16[128,128]{1,0:T(8,128)(2,1)S(1)} collective-permute-done((bf16[128,128]{1,0:T(8,128)(2,1)S(1)}, bf16[128,128]{1,0:T(8,128)(2,1)S(1)}, u32[]{:S(2)}, u32[]{:S(2)}) %collective-permute-start.22) | collective-permute-done | bytes 32800 | tf_op jit(solution)/shard_map/ppermute | solution.py:447
  58.7 1.5 %collective-permute-done.23.refs_3_ = bf16[128,128]{1,0:T(8,128)(2,1)S(1)} collective-permute-done((bf16[128,128]{1,0:T(8,128)(2,1)S(1)}, bf16[128,128]{1,0:T(8,128)(2,1)S(1)}, u32[]{:S(2)}, u32[]{:S(2)}) %collective-permute-start.23) | collective-permute-done | bytes 32800 | tf_op jit(solution)/shard_map/ppermute | solution.py:447
  60.2 0.7 %update.3 = f32[128,128]{1,0:T(8,128)} custom-call(f32[128,128]{1,0:T(8,128)S(1)} %get-tuple-element.73.volume_ref, f32[128,128]{1,0:T(8,128)S(1)} %column_weight.1.column_ref, f32[128,128]{1,0:T(8,128)S(1)} %get-tuple-element.76.refs_0_, bf16[128,128]{1,0:T(8,128)(2,1)S(1)} %collective-permute-done.20.refs_1_, ...), custom_call_target="tpu_custom_call" | custom-call | flops 4000000000 | bytes 8000000 | tf_op jit(solution)/shard_map/update/pallas_call | solution.py:432
  (54 shorter events, 9.3 us)
Async XLA Ops:
  1.1 8.3 %collective-permute-start = (bf16[160,128]{1,0:T(8,128)(2,1)S(1)}, bf16[160,128]{1,0:T(8,128)(2,1)S(1)}, u32[]{:S(2)}, u32[]{:S(2)}) collective-permute-start(bf16[160,128]{1,0:T(8,128)(2,1)S(1)} %get-tuple-element.44), channel_id=1, source_target_pairs={{0,12},{1,2},{2,1},{3,15},{4,7},{5,9},{6,10},{7,4},{8,11},{9,5},{1... | collective-permute-start | bytes 122888 | tf_op jit(solution)/shard_map/ppermute | solution.py:447
  6.2 3.4 %collective-permute-start.1 = (bf16[160,128]{1,0:T(8,128)(2,1)S(1)}, bf16[160,128]{1,0:T(8,128)(2,1)S(1)}, u32[]{:S(2)}, u32[]{:S(2)}) collective-permute-start(bf16[160,128]{1,0:T(8,128)(2,1)S(1)} %get-tuple-element.45), channel_id=1, source_target_pairs={{0,5},{1,11},{2,8},{3,6},{4,14},{5,0},{6,3},{7,13},{8,2},{9,12},{1... | collective-permute-start | bytes 122888 | tf_op jit(solution)/shard_map/ppermute | solution.py:447
  6.2 4.3 %collective-permute-start.2 = (bf16[160,128]{1,0:T(8,128)(2,1)S(1)}, bf16[160,128]{1,0:T(8,128)(2,1)S(1)}, u32[]{:S(2)}, u32[]{:S(2)}) collective-permute-start(bf16[160,128]{1,0:T(8,128)(2,1)S(1)} %get-tuple-element.46), channel_id=1, source_target_pairs={{0,9},{1,8},{2,11},{3,10},{4,13},{5,12},{6,15},{7,14},{8,1},{9,0},... | collective-permute-start | bytes 122888 | tf_op jit(solution)/shard_map/ppermute | solution.py:447
  6.6 7.8 %collective-permute-start.4 = (bf16[160,128]{1,0:T(8,128)(2,1)S(1)}, bf16[160,128]{1,0:T(8,128)(2,1)S(1)}, u32[]{:S(2)}, u32[]{:S(2)}) collective-permute-start(bf16[160,128]{1,0:T(8,128)(2,1)S(1)} %get-tuple-element.48), channel_id=1, source_target_pairs={{0,10},{1,13},{2,14},{3,9},{4,8},{5,15},{6,12},{7,11},{8,4},{9,3},... | collective-permute-start | bytes 122888 | tf_op jit(solution)/shard_map/ppermute | solution.py:447
  9.6 4.8 %collective-permute-start.3 = (bf16[480,128]{1,0:T(8,128)(2,1)S(1)}, bf16[480,128]{1,0:T(8,128)(2,1)S(1)}, u32[]{:S(2)}, u32[]{:S(2)}) collective-permute-start(bf16[480,128]{1,0:T(8,128)(2,1)S(1)} %join.2.refs_0_), channel_id=1, source_target_pairs={{0,3},{1,4},{2,7},{3,0},{4,1},{5,6},{6,5},{7,2},{8,13},{9,10},{10,... | collective-permute-start | bytes 368648 | tf_op jit(solution)/shard_map/ppermute | solution.py:447
  17.1 1.4 %collective-permute-start.5 = (f32[288,128]{1,0:T(8,128)S(1)}, f32[288,128]{1,0:T(8,128)S(1)}, u32[]{:S(2)}, u32[]{:S(2)}) collective-permute-start(f32[288,128]{1,0:T(8,128)S(1)} %forward.8), channel_id=1, source_target_pairs={{0,1},{1,0},{2,3},{3,2},{4,5},{5,4},{6,7},{7,6},{8,9},{9,8},{10,11... | collective-permute-start | bytes 442376 | tf_op jit(solution)/shard_map/ppermute | solution.py:447
  17.2 1.4 %copy-start.1 = (bf16[32,8,128]{2,1,0:T(8,128)(2,1)S(1)}, bf16[32,8,128]{2,1,0:T(8,128)(2,1)}, u32[]{:S(2)}) copy-start(bf16[32,8,128]{2,1,0:T(8,128)(2,1)} %param.7) | copy-start | bytes 196612
  18.6 1.3 %collective-permute-start.6 = (bf16[256,128]{1,0:T(8,128)(2,1)S(1)}, bf16[256,128]{1,0:T(8,128)(2,1)S(1)}, u32[]{:S(2)}, u32[]{:S(2)}) collective-permute-start(bf16[256,128]{1,0:T(8,128)(2,1)S(1)} %residual.2.refs_0_), channel_id=1, source_target_pairs={{0,1},{1,0},{2,3},{3,2},{4,5},{5,4},{6,7},{7,6},{8,9},{9,8},{10,11... | collective-permute-start | bytes 196616 | tf_op jit(solution)/shard_map/ppermute | solution.py:447
  20.8 3.8 %collective-permute-start.9 = (bf16[256,128]{1,0:T(8,128)(2,1)S(1)}, bf16[256,128]{1,0:T(8,128)(2,1)S(1)}, u32[]{:S(2)}, u32[]{:S(2)}) collective-permute-start(bf16[256,128]{1,0:T(8,128)(2,1)S(1)} %get-tuple-element.70), channel_id=1, source_target_pairs={{0,3},{1,4},{2,7},{3,0},{4,1},{5,6},{6,5},{7,2},{8,13},{9,10},{10,... | collective-permute-start | bytes 196616 | tf_op jit(solution)/shard_map/ppermute | solution.py:447
  21.7 7.2 %collective-permute-start.7 = (bf16[256,128]{1,0:T(8,128)(2,1)S(1)}, bf16[256,128]{1,0:T(8,128)(2,1)S(1)}, u32[]{:S(2)}, u32[]{:S(2)}) collective-permute-start(bf16[256,128]{1,0:T(8,128)(2,1)S(1)} %get-tuple-element.67), channel_id=1, source_target_pairs={{0,3},{1,4},{2,7},{3,0},{4,1},{5,6},{6,5},{7,2},{8,13},{9,10},{10,... | collective-permute-start | bytes 196616 | tf_op jit(solution)/shard_map/ppermute | solution.py:447
  24.6 6.1 %collective-permute-start.10 = (bf16[128,128]{1,0:T(8,128)(2,1)S(1)}, bf16[128,128]{1,0:T(8,128)(2,1)S(1)}, u32[]{:S(2)}, u32[]{:S(2)}) collective-permute-start(bf16[128,128]{1,0:T(8,128)(2,1)S(1)} %get-tuple-element.71), channel_id=1, source_target_pairs={{0,12},{1,2},{2,1},{3,15},{4,7},{5,9},{6,10},{7,4},{8,11},{9,5},{1... | collective-permute-start | bytes 98312 | tf_op jit(solution)/shard_map/ppermute | solution.py:447
  28.8 0.7 %copy-start.2 = (f32[256,4]{0,1:T(4,128)S(1)}, f32[256,4]{0,1:T(4,128)}, u32[]{:S(2)}) copy-start(f32[256,4]{0,1:T(4,128)} %param.13) | copy-start | bytes 12292
  28.8 0.7 %copy-start.3 = (f32[256,4]{0,1:T(4,128)S(1)}, f32[256,4]{0,1:T(4,128)}, u32[]{:S(2)}) copy-start(f32[256,4]{0,1:T(4,128)} %param.12) | copy-start | bytes 12292
  28.8 0.7 %copy-start.4 = (s32[256,4]{0,1:T(4,128)S(1)}, s32[256,4]{0,1:T(4,128)}, u32[]{:S(2)}) copy-start(s32[256,4]{0,1:T(4,128)} %param.9) | copy-start | bytes 12292
  28.8 4.2 %collective-permute-start.11 = (bf16[128,128]{1,0:T(8,128)(2,1)S(1)}, bf16[128,128]{1,0:T(8,128)(2,1)S(1)}, u32[]{:S(2)}, u32[]{:S(2)}) collective-permute-start(bf16[128,128]{1,0:T(8,128)(2,1)S(1)} %get-tuple-element.72), channel_id=1, source_target_pairs={{0,9},{1,8},{2,11},{3,10},{4,13},{5,12},{6,15},{7,14},{8,1},{9,0},... | collective-permute-start | bytes 98312 | tf_op jit(solution)/shard_map/ppermute | solution.py:447
  28.9 0.7 %copy-start.5 = (s32[16]{0:T(128)S(1)}, s32[16]{0:T(128)}, u32[]{:S(2)}) copy-start(s32[16]{0:T(128)} %param.11) | copy-start | bytes 196
  28.9 4.2 %copy-start = (f32[16,8,128]{2,1,0:T(8,128)S(1)}, f32[16,8,128]{2,1,0:T(8,128)}, u32[]{:S(2)}) copy-start(f32[16,8,128]{2,1,0:T(8,128)} %param.8) | copy-start | bytes 196612
  28.9 4.2 %collective-permute-start.8 = (bf16[128,128]{1,0:T(8,128)(2,1)S(1)}, bf16[128,128]{1,0:T(8,128)(2,1)S(1)}, u32[]{:S(2)}, u32[]{:S(2)}) collective-permute-start(bf16[128,128]{1,0:T(8,128)(2,1)S(1)} %get-tuple-element.69), channel_id=1, source_target_pairs={{0,5},{1,11},{2,8},{3,6},{4,14},{5,0},{6,3},{7,13},{8,2},{9,12},{1... | collective-permute-start | bytes 98312 | tf_op jit(solution)/shard_map/ppermute | solution.py:447
  33.1 6.1 %collective-permute-start.12 = (bf16[128,128]{1,0:T(8,128)(2,1)S(1)}, bf16[128,128]{1,0:T(8,128)(2,1)S(1)}, u32[]{:S(2)}, u32[]{:S(2)}) collective-permute-start(bf16[128,128]{1,0:T(8,128)(2,1)S(1)} %get-tuple-element.74.refs_0_), channel_id=1, source_target_pairs={{0,12},{1,2},{2,1},{3,15},{4,7},{5,9},{6,10},{7,4},{8,11},{9,5},{1... | collective-permute-start | bytes 98312 | tf_op jit(solution)/shard_map/ppermute | solution.py:447
  35.1 4.1 %collective-permute-start.13 = (bf16[128,128]{1,0:T(8,128)(2,1)S(1)}, bf16[128,128]{1,0:T(8,128)(2,1)S(1)}, u32[]{:S(2)}, u32[]{:S(2)}) collective-permute-start(bf16[128,128]{1,0:T(8,128)(2,1)S(1)} %get-tuple-element.74.refs_0_), channel_id=1, source_target_pairs={{0,5},{1,11},{2,8},{3,6},{4,14},{5,0},{6,3},{7,13},{8,2},{9,12},{1... | collective-permute-start | bytes 98312 | tf_op jit(solution)/shard_map/ppermute | solution.py:447
  35.3 5.1 %collective-permute-start.16 = (bf16[128,128]{1,0:T(8,128)(2,1)S(1)}, bf16[128,128]{1,0:T(8,128)(2,1)S(1)}, u32[]{:S(2)}, u32[]{:S(2)}) collective-permute-start(bf16[128,128]{1,0:T(8,128)(2,1)S(1)} %get-tuple-element.74.refs_0_), channel_id=1, source_target_pairs={{0,9},{1,8},{2,11},{3,10},{4,13},{5,12},{6,15},{7,14},{8,1},{9,0},... | collective-permute-start | bytes 98312 | tf_op jit(solution)/shard_map/ppermute | solution.py:447
  37.3 6.2 %collective-permute-start.15 = (bf16[128,128]{1,0:T(8,128)(2,1)S(1)}, bf16[128,128]{1,0:T(8,128)(2,1)S(1)}, u32[]{:S(2)}, u32[]{:S(2)}) collective-permute-start(bf16[128,128]{1,0:T(8,128)(2,1)S(1)} %get-tuple-element.74.refs_0_), channel_id=1, source_target_pairs={{0,10},{1,13},{2,14},{3,9},{4,8},{5,15},{6,12},{7,11},{8,4},{9,3},... | collective-permute-start | bytes 98312 | tf_op jit(solution)/shard_map/ppermute | solution.py:447
  39.3 4.5 %collective-permute-start.14 = (bf16[384,128]{1,0:T(8,128)(2,1)S(1)}, bf16[384,128]{1,0:T(8,128)(2,1)S(1)}, u32[]{:S(2)}, u32[]{:S(2)}) collective-permute-start(bf16[384,128]{1,0:T(8,128)(2,1)S(1)} %join.3.refs_0_), channel_id=1, source_target_pairs={{0,3},{1,4},{2,7},{3,0},{4,1},{5,6},{6,5},{7,2},{8,13},{9,10},{10,... | collective-permute-start | bytes 294920 | tf_op jit(solution)/shard_map/ppermute | solution.py:447
  44.8 2.0 %collective-permute-start.17 = (f32[256,128]{1,0:T(8,128)S(1)}, f32[256,128]{1,0:T(8,128)S(1)}, u32[]{:S(2)}, u32[]{:S(2)}) collective-permute-start(f32[256,128]{1,0:T(8,128)S(1)} %forward.11), channel_id=1, source_target_pairs={{0,1},{1,0},{2,3},{3,2},{4,5},{5,4},{6,7},{7,6},{8,9},{9,8},{10,11... | collective-permute-start | bytes 393224 | tf_op jit(solution)/shard_map/ppermute | solution.py:447
  46.9 1.3 %collective-permute-start.18 = (bf16[256,128]{1,0:T(8,128)(2,1)S(1)}, bf16[256,128]{1,0:T(8,128)(2,1)S(1)}, u32[]{:S(2)}, u32[]{:S(2)}) collective-permute-start(bf16[256,128]{1,0:T(8,128)(2,1)S(1)} %residual.3.refs_0_), channel_id=1, source_target_pairs={{0,1},{1,0},{2,3},{3,2},{4,5},{5,4},{6,7},{7,6},{8,9},{9,8},{10,11... | collective-permute-start | bytes 196616 | tf_op jit(solution)/shard_map/ppermute | solution.py:447
  49.1 3.8 %collective-permute-start.21 = (bf16[256,128]{1,0:T(8,128)(2,1)S(1)}, bf16[256,128]{1,0:T(8,128)(2,1)S(1)}, u32[]{:S(2)}, u32[]{:S(2)}) collective-permute-start(bf16[256,128]{1,0:T(8,128)(2,1)S(1)} %get-tuple-element.78), channel_id=1, source_target_pairs={{0,3},{1,4},{2,7},{3,0},{4,1},{5,6},{6,5},{7,2},{8,13},{9,10},{10,... | collective-permute-start | bytes 196616 | tf_op jit(solution)/shard_map/ppermute | solution.py:447
  49.7 7.0 %collective-permute-start.19 = (bf16[256,128]{1,0:T(8,128)(2,1)S(1)}, bf16[256,128]{1,0:T(8,128)(2,1)S(1)}, u32[]{:S(2)}, u32[]{:S(2)}) collective-permute-start(bf16[256,128]{1,0:T(8,128)(2,1)S(1)} %get-tuple-element.75), channel_id=1, source_target_pairs={{0,3},{1,4},{2,7},{3,0},{4,1},{5,6},{6,5},{7,2},{8,13},{9,10},{10,... | collective-permute-start | bytes 196616 | tf_op jit(solution)/shard_map/ppermute | solution.py:447
  52.9 5.8 %collective-permute-start.22 = (bf16[128,128]{1,0:T(8,128)(2,1)S(1)}, bf16[128,128]{1,0:T(8,128)(2,1)S(1)}, u32[]{:S(2)}, u32[]{:S(2)}) collective-permute-start(bf16[128,128]{1,0:T(8,128)(2,1)S(1)} %get-tuple-element.79), channel_id=1, source_target_pairs={{0,12},{1,2},{2,1},{3,15},{4,7},{5,9},{6,10},{7,4},{8,11},{9,5},{1... | collective-permute-start | bytes 98312 | tf_op jit(solution)/shard_map/ppermute | solution.py:447
  55.2 5.0 %collective-permute-start.23 = (bf16[128,128]{1,0:T(8,128)(2,1)S(1)}, bf16[128,128]{1,0:T(8,128)(2,1)S(1)}, u32[]{:S(2)}, u32[]{:S(2)}) collective-permute-start(bf16[128,128]{1,0:T(8,128)(2,1)S(1)} %get-tuple-element.80), channel_id=1, source_target_pairs={{0,9},{1,8},{2,11},{3,10},{4,13},{5,12},{6,15},{7,14},{8,1},{9,0},... | collective-permute-start | bytes 98312 | tf_op jit(solution)/shard_map/ppermute | solution.py:447
  56.7 3.5 %collective-permute-start.20 = (bf16[128,128]{1,0:T(8,128)(2,1)S(1)}, bf16[128,128]{1,0:T(8,128)(2,1)S(1)}, u32[]{:S(2)}, u32[]{:S(2)}) collective-permute-start(bf16[128,128]{1,0:T(8,128)(2,1)S(1)} %get-tuple-element.77), channel_id=1, source_target_pairs={{0,5},{1,11},{2,8},{3,6},{4,14},{5,0},{6,3},{7,13},{8,2},{9,12},{1... | collective-permute-start | bytes 98312 | tf_op jit(solution)/shard_map/ppermute | solution.py:447

commit v2 on v0

--- a/solution.py
+++ b/solution.py
@@ -281,10 +281,10 @@
     start_ref = None
     if start_row is not None:
         start_ref, refs = refs[0], refs[1:]
-    sum_refs, (out_ref, wide, second) = refs[:n_sums], refs[n_sums:]
+    sum_refs, (out_ref, wide) = refs[:n_sums], refs[n_sums:]
     rows = wide.shape[0] // members
     stride = sum(ref.shape[0] for ref in value_refs) // members
-    rays = second.shape[0]
+    rays = out_ref.shape[0] - (sum_refs[0].shape[0] // 2 if n_sums else 0)
     line_step = tables[0].shape[0] // depth
 
     base = 0
@@ -304,7 +304,6 @@
         else:
             lax.fori_loop(0, here, widen, 0)
         base += here
-    second[...] = jnp.zeros_like(second)
     if start_ref is None:
         out_ref[...] = jnp.zeros_like(out_ref)
     else:
@@ -333,11 +332,9 @@
             for ref, tap in zip(tables[1:], three):
                 term = spread(ref, line + level * line_step, frames) * tap
                 total = term if total is None else total + term
-        projection = (out_ref, second)[place % 2]
-        projection[tile_at(slots[1, slot], frames), :] += total.astype(BF16).astype(F32)
+        out_ref[tile_at(slots[1, slot], frames), :] += total.astype(BF16).astype(F32)
 
     for_slots(slots, one)
-    out_ref[0:rays, :] += second[...]
 
 
 def residual_kernel(frames, n_own, projection_ref, sinogram_ref, *refs):
@@ -502,7 +499,7 @@
             functools.partial(forward_kernel, sizes, len(values), members, start_row, len(sums)),
             "forward", 16 if paired else 32, [SMEM] + [VMEM] * (len(operands) - 1),
             shape((n_out + extra, extent), F32), *operands,
-            scratch=[pltpu.VMEM((members * rows, extent), F32), pltpu.VMEM((n_out, extent), F32)])
+            scratch=[pltpu.VMEM((members * rows, extent), F32)])
 
     def residual_of(projection, row_sums, *sibling):
         operands = [projection, sino, *row_sums, *sibling]

time: 60.3 us -> 60.9 us (level)
  Pallas kernels: 16.3 us -> 20 us
  starting transfers between devices: 31.2 us -> 28.6 us
  waiting for transfers between devices: 12.1 us -> 11.4 us
    pallas_call x26, Pallas kernels: 16.3 us -> 20 us  [call(): pl.pallas_call(kernel, out_shape=out_shape, in_specs=in_specs, out_specs=...]
    ppermute x24, starting transfers between devices: 31.2 us -> 28.6 us  [exchange(): lax.ppermute(values, 'slab', [(device, device ^ far[device.bit_count() %...]
    ppermute x24, waiting for transfers between devices: 12.1 us -> 11.4 us  [exchange(): lax.ppermute(values, 'slab', [(device, device ^ far[device.bit_count() %...]
  transfers between devices with their start and end apart: 24 -> 24, of which waited for: 14 -> 12; matrix products, arithmetic and copies ran while one was open for 0% -> 0% of each run, Pallas kernels for 17% -> 21%
where the time goes in v2:
time: 60.9 us; the launch traced here: 60.7 us
  starting transfers between devices  28.6 us (47%)
  Pallas kernels  20 us (33%)
  waiting for transfers between devices  11.4 us (19%)
    ppermute x24, starting transfers between devices, exchange(): lax.ppermute(values, 'slab', [(device, device ^ far[device.bit_count() %...  28.6 us
    pallas_call x26, Pallas kernels, call(): pl.pallas_call(kernel, out_shape=out_shape, in_specs=in_specs, out_specs=...  20 us
    ppermute x24, waiting for transfers between devices, exchange(): lax.ppermute(values, 'slab', [(device, device ^ far[device.bit_count() %...  11.4 us
  transfers between devices with their start and end apart: 24, of which 12 were waited for; matrix products, arithmetic and copies ran while one was open for 0% of the time, Pallas kernels for 21%

profile of v2, /device:TPU:0, one launch (start us, length us, event | category | flops | bytes accessed | tf_op | source)
XLA Modules:
  0.0 60.7 jit_solution(1242859885773150910)
XLA Ops:
  0.0 1.0 %pack.1 = (bf16[160,128]{1,0:T(8,128)(2,1)S(1)}, bf16[160,128]{1,0:T(8,128)(2,1)S(1)}, bf16[160,128]{1,0:T(8,128)(2,1)S(1)}, bf16[160,128]{1,0:T(8,128)(2,1)S(1)}, bf16[160,128]{1,0:T(8,128)(2,1)S(1)}) custom-call(f32[128,128]{1,0:T(8,128)} %bitcast.8, f32[4,256]{1,0:T(4,128)} %bitcast.12, f32[4,256]{1,0:T(4,128)} %bitcast.14, s32[4,256]{1,0:T(4,128)} %bitcast.16, ...), custom_call_target="tpu_custom_call" | custom-call | flops 4000000000 | bytes 8000000 | tf_op jit(solution)/shard_map/pack/pallas_call | solution.py:429
  1.1 3.5 %collective-permute-start = (bf16[160,128]{1,0:T(8,128)(2,1)S(1)}, bf16[160,128]{1,0:T(8,128)(2,1)S(1)}, u32[]{:S(2)}, u32[]{:S(2)}) collective-permute-start(bf16[160,128]{1,0:T(8,128)(2,1)S(1)} %get-tuple-element.44), channel_id=1, source_target_pairs={{0,9},{1,2},{2,1},{3,10},{4,7},{5,12},{6,15},{7,4},{8,11},{9,0},{1... | collective-permute-start | bytes 122888 | tf_op jit(solution)/shard_map/ppermute | solution.py:444
  4.6 1.9 %collective-permute-start.1 = (bf16[160,128]{1,0:T(8,128)(2,1)S(1)}, bf16[160,128]{1,0:T(8,128)(2,1)S(1)}, u32[]{:S(2)}, u32[]{:S(2)}) collective-permute-start(bf16[160,128]{1,0:T(8,128)(2,1)S(1)} %get-tuple-element.45), channel_id=1, source_target_pairs={{0,5},{1,8},{2,11},{3,6},{4,13},{5,0},{6,3},{7,14},{8,1},{9,12},{1... | collective-permute-start | bytes 122888 | tf_op jit(solution)/shard_map/ppermute | solution.py:444
  6.5 3.9 %collective-permute-start.4 = (bf16[160,128]{1,0:T(8,128)(2,1)S(1)}, bf16[160,128]{1,0:T(8,128)(2,1)S(1)}, u32[]{:S(2)}, u32[]{:S(2)}) collective-permute-start(bf16[160,128]{1,0:T(8,128)(2,1)S(1)} %get-tuple-element.48), channel_id=1, source_target_pairs={{0,15},{1,14},{2,13},{3,12},{4,11},{5,10},{6,9},{7,8},{8,7},{9,6},... | collective-permute-start | bytes 122888 | tf_op jit(solution)/shard_map/ppermute | solution.py:444
  10.4 1.1 %collective-permute-start.3 = (bf16[480,128]{1,0:T(8,128)(2,1)S(1)}, bf16[480,128]{1,0:T(8,128)(2,1)S(1)}, u32[]{:S(2)}, u32[]{:S(2)}) collective-permute-start(bf16[480,128]{1,0:T(8,128)(2,1)S(1)} %join.2.refs_0_), channel_id=1, source_target_pairs={{0,3},{1,4},{2,7},{3,0},{4,1},{5,6},{6,5},{7,2},{8,13},{9,10},{10,... | collective-permute-start | bytes 368648 | tf_op jit(solution)/shard_map/ppermute | solution.py:444
  12.4 1.5 %setup.2 = (s32[8,128]{1,0:T(8,128)S(4)}, f32[64,128]{1,0:T(8,128)S(1)}, s32[544,128]{1,0:T(8,128)S(1)}, f32[544,128]{1,0:T(8,128)S(1)}, f32[544,128]{1,0:T(8,12...) custom-call(bf16[480,128]{1,0:T(8,128)(2,1)S(1)} %join.2.refs_0_, ...), custom_call_target="tpu_custom_call" | custom-call | flops 4000000000 | bytes 8000000 | tf_op jit(solution)/shard_map/setup/pallas_call | solution.py:429
  13.9 1.8 %forward.6.refs_2_.refs_6_ = f32[512,128]{1,0:T(8,128)S(1)} custom-call(s32[8,128]{1,0:T(8,128)S(4)} %get-tuple-element.47.slots, bf16[480,128]{1,0:T(8,128)(2,1)S(1)} %join.2.refs_0_, bf16[160,128]{1,0:T(8,128)(2,1)S(1)} %collective-permute-done.2.refs_1_, s32[544,128]{1,0:T(8,128)S(1)} %get-tuple-element.49.refs_2_, ...), custom_call_target="tpu_custom_call" | custom-call | flops 4000000000 | bytes 8000000 | tf_op jit(solution)/shard_map/forward/pallas_call | solution.py:429
  15.7 1.6 %setup.3 = (s32[8,128]{1,0:T(8,128)S(4)}, s32[8,128]{1,0:T(8,128)S(4)}, f32[64,128]{1,0:T(8,128)S(1)}, s32[544,128]{1,0:T(8,128)S(1)}, f32[544,128]{1,0:T(8,128)...) custom-call(bf16[480,128]{1,0:T(8,128)(2,1)S(1)} %collective-permute, ...), custom_call_target="tpu_custom_call" | custom-call | flops 4000000000 | bytes 8000000 | tf_op jit(solution)/shard_map/setup/pallas_call | solution.py:429
  17.3 1.1 %forward.8 = f32[288,128]{1,0:T(8,128)S(1)} custom-call(s32[8,128]{1,0:T(8,128)S(4)} %get-tuple-element.60.slots, bf16[480,128]{1,0:T(8,128)(2,1)S(1)} %collective-permute-done.3.refs_0_, bf16[160,128]{1,0:T(8,128)(2,1)S(1)} %collective-permute-done.4.refs_1_, s32[544,128]{1,0:T(8,128)S(1)} %get-tuple-element.54.refs_2_, ...), custom_call_target="tpu_custom_call" | custom-call | flops 4000000000 | bytes 8000000 | tf_op jit(solution)/shard_map/forward/pallas_call | solution.py:429
  18.5 1.1 %forward.7.projection_ref = f32[256,128]{1,0:T(8,128)S(1)} custom-call(s32[8,128]{1,0:T(8,128)S(4)} %get-tuple-element.53.slots, bf16[480,128]{1,0:T(8,128)(2,1)S(1)} %collective-permute-done.3.refs_0_, bf16[160,128]{1,0:T(8,128)(2,1)S(1)} %collective-permute-done.4.refs_1_, s32[544,128]{1,0:T(8,128)S(1)} %get-tuple-element.54.refs_2_, ...), custom_call_target="tpu_custom_call" | custom-call | flops 4000000000 | bytes 8000000 | tf_op jit(solution)/shard_map/forward/pallas_call | solution.py:429
  20.0 0.9 %backward.7.refs_4_ = f32[512,128]{1,0:T(8,128)S(1)} custom-call(s32[8,128]{1,0:T(8,128)S(4)} %get-tuple-element.53.slots, bf16[256,128]{1,0:T(8,128)(2,1)S(1)} %residual.2.refs_0_, s32[544,128]{1,0:T(8,128)S(1)} %get-tuple-element.64.refs_1_, f32[544,128]{1,0:T(8,128)S(1)} %get-tuple-element.65.refs_2_, f32[544,128]{1,0:T(8,128)S(1)} %get-tuple-element.66.refs_3_), custom_call_target="tpu_custom_call" | custom-call | flops 4000000000 | bytes 8000000 | tf_op jit(solution)/shard_map/backward/pallas_call | solution.py:429
  21.2 0.9 %backward.8 = (bf16[256,128]{1,0:T(8,128)(2,1)S(1)}, bf16[256,128]{1,0:T(8,128)(2,1)S(1)}) custom-call(s32[8,128]{1,0:T(8,128)S(4)} %get-tuple-element.60.slots, bf16[256,128]{1,0:T(8,128)(2,1)S(1)} %collective-permute-done.6.refs_1_.refs_0_, s32[544,128]{1,0:T(8,128)S(1)} %get-tuple-element.64.refs_1_, f32[544,128]{1,0:T(8,128)S(1)} %get-tuple-element.65.refs_2_, ...), custom_call_target="tpu_custom_call" | custom-call | flops 4000000000 | bytes 8000000 | tf_op jit(solution)/shard_map/backward/pallas_call | solution.py:429
  22.1 1.7 %collective-permute-start.9 = (bf16[256,128]{1,0:T(8,128)(2,1)S(1)}, bf16[256,128]{1,0:T(8,128)(2,1)S(1)}, u32[]{:S(2)}, u32[]{:S(2)}) collective-permute-start(bf16[256,128]{1,0:T(8,128)(2,1)S(1)} %get-tuple-element.70), channel_id=1, source_target_pairs={{0,3},{1,4},{2,7},{3,0},{4,1},{5,6},{6,5},{7,2},{8,13},{9,10},{10,... | collective-permute-start | bytes 196616 | tf_op jit(solution)/shard_map/ppermute | solution.py:444
  23.9 1.5 %backward.6.sum_ref = f32[512,128]{1,0:T(8,128)S(1)} custom-call(s32[8,128]{1,0:T(8,128)S(4)} %get-tuple-element.47.slots, bf16[256,128]{1,0:T(8,128)(2,1)S(1)} %residual.2.refs_0_, bf16[256,128]{1,0:T(8,128)(2,1)S(1)} %collective-permute-done.6.refs_1_.refs_0_, s32[544,128]{1,0:T(8,128)S(1)} %get-tuple-element.61.refs_2_, ...), custom_call_target="tpu_custom_call" | custom-call | flops 4000000000 | bytes 8000000 | tf_op jit(solution)/shard_map/backward/pallas_call | solution.py:429
  25.8 1.2 %collective-permute-start.10 = (bf16[128,128]{1,0:T(8,128)(2,1)S(1)}, bf16[128,128]{1,0:T(8,128)(2,1)S(1)}, u32[]{:S(2)}, u32[]{:S(2)}) collective-permute-start(bf16[128,128]{1,0:T(8,128)(2,1)S(1)} %get-tuple-element.71), channel_id=1, source_target_pairs={{0,9},{1,2},{2,1},{3,10},{4,7},{5,12},{6,15},{7,4},{8,11},{9,0},{1... | collective-permute-start | bytes 98312 | tf_op jit(solution)/shard_map/ppermute | solution.py:444
  27.1 2.1 %collective-permute-start.11 = (bf16[128,128]{1,0:T(8,128)(2,1)S(1)}, bf16[128,128]{1,0:T(8,128)(2,1)S(1)}, u32[]{:S(2)}, u32[]{:S(2)}) collective-permute-start(bf16[128,128]{1,0:T(8,128)(2,1)S(1)} %get-tuple-element.72), channel_id=1, source_target_pairs={{0,12},{1,11},{2,8},{3,15},{4,14},{5,9},{6,10},{7,13},{8,2},{9,5},... | collective-permute-start | bytes 98312 | tf_op jit(solution)/shard_map/ppermute | solution.py:444
  30.5 2.7 %collective-permute-done.11.refs_3_ = bf16[128,128]{1,0:T(8,128)(2,1)S(1)} collective-permute-done((bf16[128,128]{1,0:T(8,128)(2,1)S(1)}, bf16[128,128]{1,0:T(8,128)(2,1)S(1)}, u32[]{:S(2)}, u32[]{:S(2)}) %collective-permute-start.11) | collective-permute-done | bytes 32800 | tf_op jit(solution)/shard_map/ppermute | solution.py:444
  33.6 1.7 %collective-permute-start.13 = (bf16[128,128]{1,0:T(8,128)(2,1)S(1)}, bf16[128,128]{1,0:T(8,128)(2,1)S(1)}, u32[]{:S(2)}, u32[]{:S(2)}) collective-permute-start(bf16[128,128]{1,0:T(8,128)(2,1)S(1)} %get-tuple-element.74.refs_0_), channel_id=1, source_target_pairs={{0,5},{1,8},{2,11},{3,6},{4,13},{5,0},{6,3},{7,14},{8,1},{9,12},{1... | collective-permute-start | bytes 98312 | tf_op jit(solution)/shard_map/ppermute | solution.py:444
  35.2 2.2 %collective-permute-start.16 = (bf16[128,128]{1,0:T(8,128)(2,1)S(1)}, bf16[128,128]{1,0:T(8,128)(2,1)S(1)}, u32[]{:S(2)}, u32[]{:S(2)}) collective-permute-start(bf16[128,128]{1,0:T(8,128)(2,1)S(1)} %get-tuple-element.74.refs_0_), channel_id=1, source_target_pairs={{0,12},{1,11},{2,8},{3,15},{4,14},{5,9},{6,10},{7,13},{8,2},{9,5},... | collective-permute-start | bytes 98312 | tf_op jit(solution)/shard_map/ppermute | solution.py:444
  37.5 0.9 %collective-permute-start.15 = (bf16[128,128]{1,0:T(8,128)(2,1)S(1)}, bf16[128,128]{1,0:T(8,128)(2,1)S(1)}, u32[]{:S(2)}, u32[]{:S(2)}) collective-permute-start(bf16[128,128]{1,0:T(8,128)(2,1)S(1)} %get-tuple-element.74.refs_0_), channel_id=1, source_target_pairs={{0,15},{1,14},{2,13},{3,12},{4,11},{5,10},{6,9},{7,8},{8,7},{9,6},... | collective-permute-start | bytes 98312 | tf_op jit(solution)/shard_map/ppermute | solution.py:444
  38.4 1.9 %collective-permute-start.14 = (bf16[384,128]{1,0:T(8,128)(2,1)S(1)}, bf16[384,128]{1,0:T(8,128)(2,1)S(1)}, u32[]{:S(2)}, u32[]{:S(2)}) collective-permute-start(bf16[384,128]{1,0:T(8,128)(2,1)S(1)} %join.3.refs_0_), channel_id=1, source_target_pairs={{0,3},{1,4},{2,7},{3,0},{4,1},{5,6},{6,5},{7,2},{8,13},{9,10},{10,... | collective-permute-start | bytes 294920 | tf_op jit(solution)/shard_map/ppermute | solution.py:444
  41.0 1.8 %forward.9.refs_6_ = f32[512,128]{1,0:T(8,128)S(1)} custom-call(s32[8,128]{1,0:T(8,128)S(4)} %get-tuple-element.47.slots, bf16[384,128]{1,0:T(8,128)(2,1)S(1)} %join.3.refs_0_, bf16[128,128]{1,0:T(8,128)(2,1)S(1)} %collective-permute-done.16.refs_1_, s32[544,128]{1,0:T(8,128)S(1)} %get-tuple-element.49.refs_2_, f32[544,128]{1,0:T(8,128)S(1)} %get-tuple-element.50.refs_3_, ...), custom_call_target="tpu_custom_call" | custom-call | flops 4000000000 | bytes 8000000 | tf_op jit(solution)/shard_map/forward/pallas_call | solution.py:429
  42.7 0.9 %collective-permute-done.15.refs_1_ = bf16[128,128]{1,0:T(8,128)(2,1)S(1)} collective-permute-done((bf16[128,128]{1,0:T(8,128)(2,1)S(1)}, bf16[128,128]{1,0:T(8,128)(2,1)S(1)}, u32[]{:S(2)}, u32[]{:S(2)}) %collective-permute-start.15) | collective-permute-done | bytes 32800 | tf_op jit(solution)/shard_map/ppermute | solution.py:444
  43.7 1.1 %forward.11 = f32[256,128]{1,0:T(8,128)S(1)} custom-call(s32[8,128]{1,0:T(8,128)S(4)} %get-tuple-element.60.slots, bf16[384,128]{1,0:T(8,128)(2,1)S(1)} %collective-permute-done.14.refs_0_, bf16[128,128]{1,0:T(8,128)(2,1)S(1)} %collective-permute-done.15.refs_1_, s32[544,128]{1,0:T(8,128)S(1)} %get-tuple-element.54.refs_2_, ...), custom_call_target="tpu_custom_call" | custom-call | flops 4000000000 | bytes 8000000 | tf_op jit(solution)/shard_map/forward/pallas_call | solution.py:429
  45.2 1.1 %forward.10.projection_ref = f32[256,128]{1,0:T(8,128)S(1)} custom-call(s32[8,128]{1,0:T(8,128)S(4)} %get-tuple-element.53.slots, bf16[384,128]{1,0:T(8,128)(2,1)S(1)} %collective-permute-done.14.refs_0_, bf16[128,128]{1,0:T(8,128)(2,1)S(1)} %collective-permute-done.15.refs_1_, s32[544,128]{1,0:T(8,128)S(1)} %get-tuple-element.54.refs_2_, ...), custom_call_target="tpu_custom_call" | custom-call | flops 4000000000 | bytes 8000000 | tf_op jit(solution)/shard_map/forward/pallas_call | solution.py:429
  47.6 0.9 %backward.11 = (bf16[256,128]{1,0:T(8,128)(2,1)S(1)}, bf16[256,128]{1,0:T(8,128)(2,1)S(1)}) custom-call(s32[8,128]{1,0:T(8,128)S(4)} %get-tuple-element.60.slots, bf16[256,128]{1,0:T(8,128)(2,1)S(1)} %collective-permute-done.18.refs_1_.refs_0_, s32[544,128]{1,0:T(8,128)S(1)} %get-tuple-element.64.refs_1_, f32[544,128]{1,0:T(8,128)S(1)} %get-tuple-element.65.refs_2_, ...), custom_call_target="tpu_custom_call" | custom-call | flops 4000000000 | bytes 8000000 | tf_op jit(solution)/shard_map/backward/pallas_call | solution.py:429
  49.4 0.9 %collective-permute-start.19 = (bf16[256,128]{1,0:T(8,128)(2,1)S(1)}, bf16[256,128]{1,0:T(8,128)(2,1)S(1)}, u32[]{:S(2)}, u32[]{:S(2)}) collective-permute-start(bf16[256,128]{1,0:T(8,128)(2,1)S(1)} %get-tuple-element.75), channel_id=1, source_target_pairs={{0,3},{1,4},{2,7},{3,0},{4,1},{5,6},{6,5},{7,2},{8,13},{9,10},{10,... | collective-permute-start | bytes 196616 | tf_op jit(solution)/shard_map/ppermute | solution.py:444
  50.3 1.5 %backward.9.sum_ref = f32[512,128]{1,0:T(8,128)S(1)} custom-call(s32[8,128]{1,0:T(8,128)S(4)} %get-tuple-element.47.slots, bf16[256,128]{1,0:T(8,128)(2,1)S(1)} %residual.3.refs_0_, bf16[256,128]{1,0:T(8,128)(2,1)S(1)} %collective-permute-done.18.refs_1_.refs_0_, s32[544,128]{1,0:T(8,128)S(1)} %get-tuple-element.61.refs_2_, ...), custom_call_target="tpu_custom_call" | custom-call | flops 4000000000 | bytes 8000000 | tf_op jit(solution)/shard_map/backward/pallas_call | solution.py:429
  52.3 1.9 %collective-permute-start.22 = (bf16[128,128]{1,0:T(8,128)(2,1)S(1)}, bf16[128,128]{1,0:T(8,128)(2,1)S(1)}, u32[]{:S(2)}, u32[]{:S(2)}) collective-permute-start(bf16[128,128]{1,0:T(8,128)(2,1)S(1)} %get-tuple-element.79), channel_id=1, source_target_pairs={{0,9},{1,2},{2,1},{3,10},{4,7},{5,12},{6,15},{7,4},{8,11},{9,0},{1... | collective-permute-start | bytes 98312 | tf_op jit(solution)/shard_map/ppermute | solution.py:444
  54.2 1.0 %collective-permute-start.23 = (bf16[128,128]{1,0:T(8,128)(2,1)S(1)}, bf16[128,128]{1,0:T(8,128)(2,1)S(1)}, u32[]{:S(2)}, u32[]{:S(2)}) collective-permute-start(bf16[128,128]{1,0:T(8,128)(2,1)S(1)} %get-tuple-element.80), channel_id=1, source_target_pairs={{0,12},{1,11},{2,8},{3,15},{4,14},{5,9},{6,10},{7,13},{8,2},{9,5},... | collective-permute-start | bytes 98312 | tf_op jit(solution)/shard_map/ppermute | solution.py:444
  55.4 1.2 %collective-permute-done.22.refs_2_ = bf16[128,128]{1,0:T(8,128)(2,1)S(1)} collective-permute-done((bf16[128,128]{1,0:T(8,128)(2,1)S(1)}, bf16[128,128]{1,0:T(8,128)(2,1)S(1)}, u32[]{:S(2)}, u32[]{:S(2)}) %collective-permute-start.22) | collective-permute-done | bytes 32800 | tf_op jit(solution)/shard_map/ppermute | solution.py:444
  56.6 3.4 %collective-permute-done.23.refs_3_ = bf16[128,128]{1,0:T(8,128)(2,1)S(1)} collective-permute-done((bf16[128,128]{1,0:T(8,128)(2,1)S(1)}, bf16[128,128]{1,0:T(8,128)(2,1)S(1)}, u32[]{:S(2)}, u32[]{:S(2)}) %collective-permute-start.23) | collective-permute-done | bytes 32800 | tf_op jit(solution)/shard_map/ppermute | solution.py:444
  (54 shorter events, 8.6 us)
Async XLA Ops:
  1.1 9.3 %collective-permute-start = (bf16[160,128]{1,0:T(8,128)(2,1)S(1)}, bf16[160,128]{1,0:T(8,128)(2,1)S(1)}, u32[]{:S(2)}, u32[]{:S(2)}) collective-permute-start(bf16[160,128]{1,0:T(8,128)(2,1)S(1)} %get-tuple-element.44), channel_id=1, source_target_pairs={{0,9},{1,2},{2,1},{3,10},{4,7},{5,12},{6,15},{7,4},{8,11},{9,0},{1... | collective-permute-start | bytes 122888 | tf_op jit(solution)/shard_map/ppermute | solution.py:444
  4.6 5.8 %collective-permute-start.1 = (bf16[160,128]{1,0:T(8,128)(2,1)S(1)}, bf16[160,128]{1,0:T(8,128)(2,1)S(1)}, u32[]{:S(2)}, u32[]{:S(2)}) collective-permute-start(bf16[160,128]{1,0:T(8,128)(2,1)S(1)} %get-tuple-element.45), channel_id=1, source_target_pairs={{0,5},{1,8},{2,11},{3,6},{4,13},{5,0},{6,3},{7,14},{8,1},{9,12},{1... | collective-permute-start | bytes 122888 | tf_op jit(solution)/shard_map/ppermute | solution.py:444
  6.5 5.9 %collective-permute-start.2 = (bf16[160,128]{1,0:T(8,128)(2,1)S(1)}, bf16[160,128]{1,0:T(8,128)(2,1)S(1)}, u32[]{:S(2)}, u32[]{:S(2)}) collective-permute-start(bf16[160,128]{1,0:T(8,128)(2,1)S(1)} %get-tuple-element.46), channel_id=1, source_target_pairs={{0,12},{1,11},{2,8},{3,15},{4,14},{5,9},{6,10},{7,13},{8,2},{9,5},... | collective-permute-start | bytes 122888 | tf_op jit(solution)/shard_map/ppermute | solution.py:444
  6.5 9.2 %collective-permute-start.4 = (bf16[160,128]{1,0:T(8,128)(2,1)S(1)}, bf16[160,128]{1,0:T(8,128)(2,1)S(1)}, u32[]{:S(2)}, u32[]{:S(2)}) collective-permute-start(bf16[160,128]{1,0:T(8,128)(2,1)S(1)} %get-tuple-element.48), channel_id=1, source_target_pairs={{0,15},{1,14},{2,13},{3,12},{4,11},{5,10},{6,9},{7,8},{8,7},{9,6},... | collective-permute-start | bytes 122888 | tf_op jit(solution)/shard_map/ppermute | solution.py:444
  10.4 5.2 %collective-permute-start.3 = (bf16[480,128]{1,0:T(8,128)(2,1)S(1)}, bf16[480,128]{1,0:T(8,128)(2,1)S(1)}, u32[]{:S(2)}, u32[]{:S(2)}) collective-permute-start(bf16[480,128]{1,0:T(8,128)(2,1)S(1)} %join.2.refs_0_), channel_id=1, source_target_pairs={{0,3},{1,4},{2,7},{3,0},{4,1},{5,6},{6,5},{7,2},{8,13},{9,10},{10,... | collective-permute-start | bytes 368648 | tf_op jit(solution)/shard_map/ppermute | solution.py:444
  18.4 1.4 %collective-permute-start.5 = (f32[288,128]{1,0:T(8,128)S(1)}, f32[288,128]{1,0:T(8,128)S(1)}, u32[]{:S(2)}, u32[]{:S(2)}) collective-permute-start(f32[288,128]{1,0:T(8,128)S(1)} %forward.8), channel_id=1, source_target_pairs={{0,1},{1,0},{2,3},{3,2},{4,5},{5,4},{6,7},{7,6},{8,9},{9,8},{10,11... | collective-permute-start | bytes 442376 | tf_op jit(solution)/shard_map/ppermute | solution.py:444
  18.4 1.4 %copy-start.1 = (bf16[32,8,128]{2,1,0:T(8,128)(2,1)S(1)}, bf16[32,8,128]{2,1,0:T(8,128)(2,1)}, u32[]{:S(2)}) copy-start(bf16[32,8,128]{2,1,0:T(8,128)(2,1)} %param.7) | copy-start | bytes 196612
  19.8 1.3 %collective-permute-start.6 = (bf16[256,128]{1,0:T(8,128)(2,1)S(1)}, bf16[256,128]{1,0:T(8,128)(2,1)S(1)}, u32[]{:S(2)}, u32[]{:S(2)}) collective-permute-start(bf16[256,128]{1,0:T(8,128)(2,1)S(1)} %residual.2.refs_0_), channel_id=1, source_target_pairs={{0,1},{1,0},{2,3},{3,2},{4,5},{5,4},{6,7},{7,6},{8,9},{9,8},{10,11... | collective-permute-start | bytes 196616 | tf_op jit(solution)/shard_map/ppermute | solution.py:444
  22.1 3.8 %collective-permute-start.9 = (bf16[256,128]{1,0:T(8,128)(2,1)S(1)}, bf16[256,128]{1,0:T(8,128)(2,1)S(1)}, u32[]{:S(2)}, u32[]{:S(2)}) collective-permute-start(bf16[256,128]{1,0:T(8,128)(2,1)S(1)} %get-tuple-element.70), channel_id=1, source_target_pairs={{0,3},{1,4},{2,7},{3,0},{4,1},{5,6},{6,5},{7,2},{8,13},{9,10},{10,... | collective-permute-start | bytes 196616 | tf_op jit(solution)/shard_map/ppermute | solution.py:444
  23.7 5.4 %collective-permute-start.7 = (bf16[256,128]{1,0:T(8,128)(2,1)S(1)}, bf16[256,128]{1,0:T(8,128)(2,1)S(1)}, u32[]{:S(2)}, u32[]{:S(2)}) collective-permute-start(bf16[256,128]{1,0:T(8,128)(2,1)S(1)} %get-tuple-element.67), channel_id=1, source_target_pairs={{0,3},{1,4},{2,7},{3,0},{4,1},{5,6},{6,5},{7,2},{8,13},{9,10},{10,... | collective-permute-start | bytes 196616 | tf_op jit(solution)/shard_map/ppermute | solution.py:444
  25.8 4.6 %collective-permute-start.10 = (bf16[128,128]{1,0:T(8,128)(2,1)S(1)}, bf16[128,128]{1,0:T(8,128)(2,1)S(1)}, u32[]{:S(2)}, u32[]{:S(2)}) collective-permute-start(bf16[128,128]{1,0:T(8,128)(2,1)S(1)} %get-tuple-element.71), channel_id=1, source_target_pairs={{0,9},{1,2},{2,1},{3,10},{4,7},{5,12},{6,15},{7,4},{8,11},{9,0},{1... | collective-permute-start | bytes 98312 | tf_op jit(solution)/shard_map/ppermute | solution.py:444
  27.1 2.2 %copy-start.2 = (f32[256,4]{0,1:T(4,128)S(1)}, f32[256,4]{0,1:T(4,128)}, u32[]{:S(2)}) copy-start(f32[256,4]{0,1:T(4,128)} %param.13) | copy-start | bytes 12292
  27.1 2.2 %copy-start.3 = (f32[256,4]{0,1:T(4,128)S(1)}, f32[256,4]{0,1:T(4,128)}, u32[]{:S(2)}) copy-start(f32[256,4]{0,1:T(4,128)} %param.12) | copy-start | bytes 12292
  27.1 2.2 %copy-start.4 = (s32[256,4]{0,1:T(4,128)S(1)}, s32[256,4]{0,1:T(4,128)}, u32[]{:S(2)}) copy-start(s32[256,4]{0,1:T(4,128)} %param.9) | copy-start | bytes 12292
  27.1 6.1 %collective-permute-start.11 = (bf16[128,128]{1,0:T(8,128)(2,1)S(1)}, bf16[128,128]{1,0:T(8,128)(2,1)S(1)}, u32[]{:S(2)}, u32[]{:S(2)}) collective-permute-start(bf16[128,128]{1,0:T(8,128)(2,1)S(1)} %get-tuple-element.72), channel_id=1, source_target_pairs={{0,12},{1,11},{2,8},{3,15},{4,14},{5,9},{6,10},{7,13},{8,2},{9,5},... | collective-permute-start | bytes 98312 | tf_op jit(solution)/shard_map/ppermute | solution.py:444
  29.2 0.7 %copy-start.5 = (s32[16]{0:T(128)S(1)}, s32[16]{0:T(128)}, u32[]{:S(2)}) copy-start(s32[16]{0:T(128)} %param.11) | copy-start | bytes 196
  29.2 4.1 %copy-start = (f32[16,8,128]{2,1,0:T(8,128)S(1)}, f32[16,8,128]{2,1,0:T(8,128)}, u32[]{:S(2)}) copy-start(f32[16,8,128]{2,1,0:T(8,128)} %param.8) | copy-start | bytes 196612
  29.2 4.1 %collective-permute-start.8 = (bf16[128,128]{1,0:T(8,128)(2,1)S(1)}, bf16[128,128]{1,0:T(8,128)(2,1)S(1)}, u32[]{:S(2)}, u32[]{:S(2)}) collective-permute-start(bf16[128,128]{1,0:T(8,128)(2,1)S(1)} %get-tuple-element.69), channel_id=1, source_target_pairs={{0,5},{1,8},{2,11},{3,6},{4,13},{5,0},{6,3},{7,14},{8,1},{9,12},{1... | collective-permute-start | bytes 98312 | tf_op jit(solution)/shard_map/ppermute | solution.py:444
  33.3 5.1 %collective-permute-start.12 = (bf16[128,128]{1,0:T(8,128)(2,1)S(1)}, bf16[128,128]{1,0:T(8,128)(2,1)S(1)}, u32[]{:S(2)}, u32[]{:S(2)}) collective-permute-start(bf16[128,128]{1,0:T(8,128)(2,1)S(1)} %get-tuple-element.74.refs_0_), channel_id=1, source_target_pairs={{0,9},{1,2},{2,1},{3,10},{4,7},{5,12},{6,15},{7,4},{8,11},{9,0},{1... | collective-permute-start | bytes 98312 | tf_op jit(solution)/shard_map/ppermute | solution.py:444
  33.6 4.8 %collective-permute-start.13 = (bf16[128,128]{1,0:T(8,128)(2,1)S(1)}, bf16[128,128]{1,0:T(8,128)(2,1)S(1)}, u32[]{:S(2)}, u32[]{:S(2)}) collective-permute-start(bf16[128,128]{1,0:T(8,128)(2,1)S(1)} %get-tuple-element.74.refs_0_), channel_id=1, source_target_pairs={{0,5},{1,8},{2,11},{3,6},{4,13},{5,0},{6,3},{7,14},{8,1},{9,12},{1... | collective-permute-start | bytes 98312 | tf_op jit(solution)/shard_map/ppermute | solution.py:444
  35.2 5.7 %collective-permute-start.16 = (bf16[128,128]{1,0:T(8,128)(2,1)S(1)}, bf16[128,128]{1,0:T(8,128)(2,1)S(1)}, u32[]{:S(2)}, u32[]{:S(2)}) collective-permute-start(bf16[128,128]{1,0:T(8,128)(2,1)S(1)} %get-tuple-element.74.refs_0_), channel_id=1, source_target_pairs={{0,12},{1,11},{2,8},{3,15},{4,14},{5,9},{6,10},{7,13},{8,2},{9,5},... | collective-permute-start | bytes 98312 | tf_op jit(solution)/shard_map/ppermute | solution.py:444
  37.5 6.2 %collective-permute-start.15 = (bf16[128,128]{1,0:T(8,128)(2,1)S(1)}, bf16[128,128]{1,0:T(8,128)(2,1)S(1)}, u32[]{:S(2)}, u32[]{:S(2)}) collective-permute-start(bf16[128,128]{1,0:T(8,128)(2,1)S(1)} %get-tuple-element.74.refs_0_), channel_id=1, source_target_pairs={{0,15},{1,14},{2,13},{3,12},{4,11},{5,10},{6,9},{7,8},{8,7},{9,6},... | collective-permute-start | bytes 98312 | tf_op jit(solution)/shard_map/ppermute | solution.py:444
  38.4 5.3 %collective-permute-start.14 = (bf16[384,128]{1,0:T(8,128)(2,1)S(1)}, bf16[384,128]{1,0:T(8,128)(2,1)S(1)}, u32[]{:S(2)}, u32[]{:S(2)}) collective-permute-start(bf16[384,128]{1,0:T(8,128)(2,1)S(1)} %join.3.refs_0_), channel_id=1, source_target_pairs={{0,3},{1,4},{2,7},{3,0},{4,1},{5,6},{6,5},{7,2},{8,13},{9,10},{10,... | collective-permute-start | bytes 294920 | tf_op jit(solution)/shard_map/ppermute | solution.py:444
  44.8 1.5 %collective-permute-start.17 = (f32[256,128]{1,0:T(8,128)S(1)}, f32[256,128]{1,0:T(8,128)S(1)}, u32[]{:S(2)}, u32[]{:S(2)}) collective-permute-start(f32[256,128]{1,0:T(8,128)S(1)} %forward.11), channel_id=1, source_target_pairs={{0,1},{1,0},{2,3},{3,2},{4,5},{5,4},{6,7},{7,6},{8,9},{9,8},{10,11... | collective-permute-start | bytes 393224 | tf_op jit(solution)/shard_map/ppermute | solution.py:444
  46.3 1.3 %collective-permute-start.18 = (bf16[256,128]{1,0:T(8,128)(2,1)S(1)}, bf16[256,128]{1,0:T(8,128)(2,1)S(1)}, u32[]{:S(2)}, u32[]{:S(2)}) collective-permute-start(bf16[256,128]{1,0:T(8,128)(2,1)S(1)} %residual.3.refs_0_), channel_id=1, source_target_pairs={{0,1},{1,0},{2,3},{3,2},{4,5},{5,4},{6,7},{7,6},{8,9},{9,8},{10,11... | collective-permute-start | bytes 196616 | tf_op jit(solution)/shard_map/ppermute | solution.py:444
  48.5 3.8 %collective-permute-start.21 = (bf16[256,128]{1,0:T(8,128)(2,1)S(1)}, bf16[256,128]{1,0:T(8,128)(2,1)S(1)}, u32[]{:S(2)}, u32[]{:S(2)}) collective-permute-start(bf16[256,128]{1,0:T(8,128)(2,1)S(1)} %get-tuple-element.78), channel_id=1, source_target_pairs={{0,3},{1,4},{2,7},{3,0},{4,1},{5,6},{6,5},{7,2},{8,13},{9,10},{10,... | collective-permute-start | bytes 196616 | tf_op jit(solution)/shard_map/ppermute | solution.py:444
  49.4 5.7 %collective-permute-start.19 = (bf16[256,128]{1,0:T(8,128)(2,1)S(1)}, bf16[256,128]{1,0:T(8,128)(2,1)S(1)}, u32[]{:S(2)}, u32[]{:S(2)}) collective-permute-start(bf16[256,128]{1,0:T(8,128)(2,1)S(1)} %get-tuple-element.75), channel_id=1, source_target_pairs={{0,3},{1,4},{2,7},{3,0},{4,1},{5,6},{6,5},{7,2},{8,13},{9,10},{10,... | collective-permute-start | bytes 196616 | tf_op jit(solution)/shard_map/ppermute | solution.py:444
  52.3 4.3 %collective-permute-start.22 = (bf16[128,128]{1,0:T(8,128)(2,1)S(1)}, bf16[128,128]{1,0:T(8,128)(2,1)S(1)}, u32[]{:S(2)}, u32[]{:S(2)}) collective-permute-start(bf16[128,128]{1,0:T(8,128)(2,1)S(1)} %get-tuple-element.79), channel_id=1, source_target_pairs={{0,9},{1,2},{2,1},{3,10},{4,7},{5,12},{6,15},{7,4},{8,11},{9,0},{1... | collective-permute-start | bytes 98312 | tf_op jit(solution)/shard_map/ppermute | solution.py:444
  54.2 5.9 %collective-permute-start.23 = (bf16[128,128]{1,0:T(8,128)(2,1)S(1)}, bf16[128,128]{1,0:T(8,128)(2,1)S(1)}, u32[]{:S(2)}, u32[]{:S(2)}) collective-permute-start(bf16[128,128]{1,0:T(8,128)(2,1)S(1)} %get-tuple-element.80), channel_id=1, source_target_pairs={{0,12},{1,11},{2,8},{3,15},{4,14},{5,9},{6,10},{7,13},{8,2},{9,5},... | collective-permute-start | bytes 98312 | tf_op jit(solution)/shard_map/ppermute | solution.py:444
  55.2 4.9 %collective-permute-start.20 = (bf16[128,128]{1,0:T(8,128)(2,1)S(1)}, bf16[128,128]{1,0:T(8,128)(2,1)S(1)}, u32[]{:S(2)}, u32[]{:S(2)}) collective-permute-start(bf16[128,128]{1,0:T(8,128)(2,1)S(1)} %get-tuple-element.77), channel_id=1, source_target_pairs={{0,5},{1,8},{2,11},{3,6},{4,13},{5,0},{6,3},{7,14},{8,1},{9,12},{1... | collective-permute-start | bytes 98312 | tf_op jit(solution)/shard_map/ppermute | solution.py:444

commit v3 on v0

--- a/solution.py
+++ b/solution.py
@@ -459,7 +459,7 @@
     sizes = (capacity, depth, frames)
     paired = n_slab == 16
     span = 2 if paired else 1
-    n_bank = 2 if paired else 1
+    n_bank = 4 if paired else 1
     shape = jax.ShapeDtypeStruct
     n_rays = ray_tiles * frames
     volume = start_volume.reshape(rows, extent)

time: 60.3 us -> 60.9 us (level)
  Pallas kernels: 16.3 us -> 19 us
  starting transfers between devices: 31.2 us -> 29.7 us
  waiting for transfers between devices: 12.1 us -> 10.9 us
    pallas_call x26, Pallas kernels: 16.3 us -> 19 us  [call(): pl.pallas_call(kernel, out_shape=out_shape, in_specs=in_specs, out_specs=...]
    ppermute x24, starting transfers between devices: 31.2 us -> 29.7 us  [exchange(): lax.ppermute(values, 'slab', [(device, device ^ far[device.bit_count() %...]
    ppermute x24, waiting for transfers between devices: 12.1 us -> 10.9 us  [exchange(): lax.ppermute(values, 'slab', [(device, device ^ far[device.bit_count() %...]
  transfers between devices with their start and end apart: 24 -> 24, of which waited for: 14 -> 13; matrix products, arithmetic and copies ran while one was open for 0% -> 0% of each run, Pallas kernels for 17% -> 19%
where the time goes in v3:
time: 60.9 us; the launch traced here: 60.4 us
  starting transfers between devices  29.7 us (49%)
  Pallas kernels  19 us (31%)
  waiting for transfers between devices  10.9 us (18%)
    ppermute x24, starting transfers between devices, exchange(): lax.ppermute(values, 'slab', [(device, device ^ far[device.bit_count() %...  29.7 us
    pallas_call x26, Pallas kernels, call(): pl.pallas_call(kernel, out_shape=out_shape, in_specs=in_specs, out_specs=...  19 us
    ppermute x24, waiting for transfers between devices, exchange(): lax.ppermute(values, 'slab', [(device, device ^ far[device.bit_count() %...  10.9 us
  transfers between devices with their start and end apart: 24, of which 13 were waited for; matrix products, arithmetic and copies ran while one was open for 0% of the time, Pallas kernels for 19%

profile of v3, /device:TPU:0, one launch (start us, length us, event | category | flops | bytes accessed | tf_op | source)
XLA Modules:
  0.0 60.4 jit_solution(16374659755577525809)
XLA Ops:
  0.0 1.0 %pack.1 = (bf16[160,128]{1,0:T(8,128)(2,1)S(1)}, bf16[160,128]{1,0:T(8,128)(2,1)S(1)}, bf16[160,128]{1,0:T(8,128)(2,1)S(1)}, bf16[160,128]{1,0:T(8,128)(2,1)S(1)}, bf16[160,128]{1,0:T(8,128)(2,1)S(1)}) custom-call(f32[128,128]{1,0:T(8,128)} %bitcast.8, f32[4,256]{1,0:T(4,128)} %bitcast.12, f32[4,256]{1,0:T(4,128)} %bitcast.14, s32[4,256]{1,0:T(4,128)} %bitcast.16, ...), custom_call_target="tpu_custom_call" | custom-call | flops 4000000000 | bytes 8000000 | tf_op jit(solution)/shard_map/pack/pallas_call | solution.py:432
  1.1 3.5 %collective-permute-start = (bf16[160,128]{1,0:T(8,128)(2,1)S(1)}, bf16[160,128]{1,0:T(8,128)(2,1)S(1)}, u32[]{:S(2)}, u32[]{:S(2)}) collective-permute-start(bf16[160,128]{1,0:T(8,128)(2,1)S(1)} %get-tuple-element.44), channel_id=1, source_target_pairs={{0,9},{1,2},{2,1},{3,10},{4,7},{5,12},{6,15},{7,4},{8,11},{9,0},{1... | collective-permute-start | bytes 122888 | tf_op jit(solution)/shard_map/ppermute | solution.py:447
  4.6 1.9 %collective-permute-start.1 = (bf16[160,128]{1,0:T(8,128)(2,1)S(1)}, bf16[160,128]{1,0:T(8,128)(2,1)S(1)}, u32[]{:S(2)}, u32[]{:S(2)}) collective-permute-start(bf16[160,128]{1,0:T(8,128)(2,1)S(1)} %get-tuple-element.45), channel_id=1, source_target_pairs={{0,5},{1,8},{2,11},{3,6},{4,13},{5,0},{6,3},{7,14},{8,1},{9,12},{1... | collective-permute-start | bytes 122888 | tf_op jit(solution)/shard_map/ppermute | solution.py:447
  6.5 3.9 %collective-permute-start.4 = (bf16[160,128]{1,0:T(8,128)(2,1)S(1)}, bf16[160,128]{1,0:T(8,128)(2,1)S(1)}, u32[]{:S(2)}, u32[]{:S(2)}) collective-permute-start(bf16[160,128]{1,0:T(8,128)(2,1)S(1)} %get-tuple-element.48), channel_id=1, source_target_pairs={{0,15},{1,14},{2,13},{3,12},{4,11},{5,10},{6,9},{7,8},{8,7},{9,6},... | collective-permute-start | bytes 122888 | tf_op jit(solution)/shard_map/ppermute | solution.py:447
  10.4 1.1 %collective-permute-start.3 = (bf16[480,128]{1,0:T(8,128)(2,1)S(1)}, bf16[480,128]{1,0:T(8,128)(2,1)S(1)}, u32[]{:S(2)}, u32[]{:S(2)}) collective-permute-start(bf16[480,128]{1,0:T(8,128)(2,1)S(1)} %join.2.refs_0_), channel_id=1, source_target_pairs={{0,3},{1,4},{2,7},{3,0},{4,1},{5,6},{6,5},{7,2},{8,13},{9,10},{10,... | collective-permute-start | bytes 368648 | tf_op jit(solution)/shard_map/ppermute | solution.py:447
  11.5 0.8 %collective-permute-done.2.refs_1_ = bf16[160,128]{1,0:T(8,128)(2,1)S(1)} collective-permute-done((bf16[160,128]{1,0:T(8,128)(2,1)S(1)}, bf16[160,128]{1,0:T(8,128)(2,1)S(1)}, u32[]{:S(2)}, u32[]{:S(2)}) %collective-permute-start.2) | collective-permute-done | bytes 40992 | tf_op jit(solution)/shard_map/ppermute | solution.py:447
  12.4 1.5 %setup.2 = (s32[8,128]{1,0:T(8,128)S(4)}, f32[64,128]{1,0:T(8,128)S(1)}, s32[544,128]{1,0:T(8,128)S(1)}, f32[544,128]{1,0:T(8,128)S(1)}, f32[544,128]{1,0:T(8,12...) custom-call(bf16[480,128]{1,0:T(8,128)(2,1)S(1)} %join.2.refs_0_, ...), custom_call_target="tpu_custom_call" | custom-call | flops 4000000000 | bytes 8000000 | tf_op jit(solution)/shard_map/setup/pallas_call | solution.py:432
  13.9 1.8 %forward.6.refs_2_.refs_6_ = f32[512,128]{1,0:T(8,128)S(1)} custom-call(s32[8,128]{1,0:T(8,128)S(4)} %get-tuple-element.47.slots, bf16[480,128]{1,0:T(8,128)(2,1)S(1)} %join.2.refs_0_, bf16[160,128]{1,0:T(8,128)(2,1)S(1)} %collective-permute-done.2.refs_1_, s32[544,128]{1,0:T(8,128)S(1)} %get-tuple-element.49.refs_2_, ...), custom_call_target="tpu_custom_call" | custom-call | flops 4000000000 | bytes 8000000 | tf_op jit(solution)/shard_map/forward/pallas_call | solution.py:432
  15.7 1.6 %setup.3 = (s32[8,128]{1,0:T(8,128)S(4)}, s32[8,128]{1,0:T(8,128)S(4)}, f32[64,128]{1,0:T(8,128)S(1)}, s32[544,128]{1,0:T(8,128)S(1)}, f32[544,128]{1,0:T(8,128)...) custom-call(bf16[480,128]{1,0:T(8,128)(2,1)S(1)} %collective-permute, ...), custom_call_target="tpu_custom_call" | custom-call | flops 4000000000 | bytes 8000000 | tf_op jit(solution)/shard_map/setup/pallas_call | solution.py:432
  17.3 1.1 %forward.8 = f32[288,128]{1,0:T(8,128)S(1)} custom-call(s32[8,128]{1,0:T(8,128)S(4)} %get-tuple-element.60.slots, bf16[480,128]{1,0:T(8,128)(2,1)S(1)} %collective-permute-done.3.refs_0_, bf16[160,128]{1,0:T(8,128)(2,1)S(1)} %collective-permute-done.4.refs_1_, s32[544,128]{1,0:T(8,128)S(1)} %get-tuple-element.54.refs_2_, ...), custom_call_target="tpu_custom_call" | custom-call | flops 4000000000 | bytes 8000000 | tf_op jit(solution)/shard_map/forward/pallas_call | solution.py:432
  18.5 0.7 %forward.7.projection_ref = f32[256,128]{1,0:T(8,128)S(1)} custom-call(s32[8,128]{1,0:T(8,128)S(4)} %get-tuple-element.53.slots, bf16[480,128]{1,0:T(8,128)(2,1)S(1)} %collective-permute-done.3.refs_0_, bf16[160,128]{1,0:T(8,128)(2,1)S(1)} %collective-permute-done.4.refs_1_, s32[544,128]{1,0:T(8,128)S(1)} %get-tuple-element.54.refs_2_, ...), custom_call_target="tpu_custom_call" | custom-call | flops 4000000000 | bytes 8000000 | tf_op jit(solution)/shard_map/forward/pallas_call | solution.py:432
  21.2 0.9 %backward.8 = (bf16[256,128]{1,0:T(8,128)(2,1)S(1)}, bf16[256,128]{1,0:T(8,128)(2,1)S(1)}) custom-call(s32[8,128]{1,0:T(8,128)S(4)} %get-tuple-element.60.slots, bf16[256,128]{1,0:T(8,128)(2,1)S(1)} %collective-permute-done.6.refs_1_.refs_0_, s32[544,128]{1,0:T(8,128)S(1)} %get-tuple-element.64.refs_1_, f32[544,128]{1,0:T(8,128)S(1)} %get-tuple-element.65.refs_2_, ...), custom_call_target="tpu_custom_call" | custom-call | flops 4000000000 | bytes 8000000 | tf_op jit(solution)/shard_map/backward/pallas_call | solution.py:432
  22.2 2.3 %collective-permute-start.9 = (bf16[256,128]{1,0:T(8,128)(2,1)S(1)}, bf16[256,128]{1,0:T(8,128)(2,1)S(1)}, u32[]{:S(2)}, u32[]{:S(2)}) collective-permute-start(bf16[256,128]{1,0:T(8,128)(2,1)S(1)} %get-tuple-element.70), channel_id=1, source_target_pairs={{0,3},{1,4},{2,7},{3,0},{4,1},{5,6},{6,5},{7,2},{8,13},{9,10},{10,... | collective-permute-start | bytes 196616 | tf_op jit(solution)/shard_map/ppermute | solution.py:447
  24.6 1.5 %backward.6.sum_ref = f32[512,128]{1,0:T(8,128)S(1)} custom-call(s32[8,128]{1,0:T(8,128)S(4)} %get-tuple-element.47.slots, bf16[256,128]{1,0:T(8,128)(2,1)S(1)} %residual.2.refs_0_, bf16[256,128]{1,0:T(8,128)(2,1)S(1)} %collective-permute-done.6.refs_1_.refs_0_, s32[544,128]{1,0:T(8,128)S(1)} %get-tuple-element.61.refs_2_, ...), custom_call_target="tpu_custom_call" | custom-call | flops 4000000000 | bytes 8000000 | tf_op jit(solution)/shard_map/backward/pallas_call | solution.py:432
  26.6 3.1 %collective-permute-start.11 = (bf16[128,128]{1,0:T(8,128)(2,1)S(1)}, bf16[128,128]{1,0:T(8,128)(2,1)S(1)}, u32[]{:S(2)}, u32[]{:S(2)}) collective-permute-start(bf16[128,128]{1,0:T(8,128)(2,1)S(1)} %get-tuple-element.72), channel_id=1, source_target_pairs={{0,12},{1,11},{2,8},{3,15},{4,14},{5,9},{6,10},{7,13},{8,2},{9,5},... | collective-permute-start | bytes 98312 | tf_op jit(solution)/shard_map/ppermute | solution.py:447
  31.0 1.7 %collective-permute-done.11.refs_3_ = bf16[128,128]{1,0:T(8,128)(2,1)S(1)} collective-permute-done((bf16[128,128]{1,0:T(8,128)(2,1)S(1)}, bf16[128,128]{1,0:T(8,128)(2,1)S(1)}, u32[]{:S(2)}, u32[]{:S(2)}) %collective-permute-start.11) | collective-permute-done | bytes 32800 | tf_op jit(solution)/shard_map/ppermute | solution.py:447
  32.7 1.0 %collective-permute-done.8.refs_1_ = bf16[128,128]{1,0:T(8,128)(2,1)S(1)} collective-permute-done((bf16[128,128]{1,0:T(8,128)(2,1)S(1)}, bf16[128,128]{1,0:T(8,128)(2,1)S(1)}, u32[]{:S(2)}, u32[]{:S(2)}) %collective-permute-start.8) | collective-permute-done | bytes 32800 | tf_op jit(solution)/shard_map/ppermute | solution.py:447
  33.8 2.0 %collective-permute-start.13 = (bf16[128,128]{1,0:T(8,128)(2,1)S(1)}, bf16[128,128]{1,0:T(8,128)(2,1)S(1)}, u32[]{:S(2)}, u32[]{:S(2)}) collective-permute-start(bf16[128,128]{1,0:T(8,128)(2,1)S(1)} %get-tuple-element.74.refs_0_), channel_id=1, source_target_pairs={{0,5},{1,8},{2,11},{3,6},{4,13},{5,0},{6,3},{7,14},{8,1},{9,12},{1... | collective-permute-start | bytes 98312 | tf_op jit(solution)/shard_map/ppermute | solution.py:447
  35.8 2.1 %collective-permute-start.16 = (bf16[128,128]{1,0:T(8,128)(2,1)S(1)}, bf16[128,128]{1,0:T(8,128)(2,1)S(1)}, u32[]{:S(2)}, u32[]{:S(2)}) collective-permute-start(bf16[128,128]{1,0:T(8,128)(2,1)S(1)} %get-tuple-element.74.refs_0_), channel_id=1, source_target_pairs={{0,12},{1,11},{2,8},{3,15},{4,14},{5,9},{6,10},{7,13},{8,2},{9,5},... | collective-permute-start | bytes 98312 | tf_op jit(solution)/shard_map/ppermute | solution.py:447
  37.9 1.1 %collective-permute-start.15 = (bf16[128,128]{1,0:T(8,128)(2,1)S(1)}, bf16[128,128]{1,0:T(8,128)(2,1)S(1)}, u32[]{:S(2)}, u32[]{:S(2)}) collective-permute-start(bf16[128,128]{1,0:T(8,128)(2,1)S(1)} %get-tuple-element.74.refs_0_), channel_id=1, source_target_pairs={{0,15},{1,14},{2,13},{3,12},{4,11},{5,10},{6,9},{7,8},{8,7},{9,6},... | collective-permute-start | bytes 98312 | tf_op jit(solution)/shard_map/ppermute | solution.py:447
  39.0 1.9 %collective-permute-start.14 = (bf16[384,128]{1,0:T(8,128)(2,1)S(1)}, bf16[384,128]{1,0:T(8,128)(2,1)S(1)}, u32[]{:S(2)}, u32[]{:S(2)}) collective-permute-start(bf16[384,128]{1,0:T(8,128)(2,1)S(1)} %join.3.refs_0_), channel_id=1, source_target_pairs={{0,3},{1,4},{2,7},{3,0},{4,1},{5,6},{6,5},{7,2},{8,13},{9,10},{10,... | collective-permute-start | bytes 294920 | tf_op jit(solution)/shard_map/ppermute | solution.py:447
  41.6 1.8 %forward.9.refs_6_ = f32[512,128]{1,0:T(8,128)S(1)} custom-call(s32[8,128]{1,0:T(8,128)S(4)} %get-tuple-element.47.slots, bf16[384,128]{1,0:T(8,128)(2,1)S(1)} %join.3.refs_0_, bf16[128,128]{1,0:T(8,128)(2,1)S(1)} %collective-permute-done.16.refs_1_, s32[544,128]{1,0:T(8,128)S(1)} %get-tuple-element.49.refs_2_, f32[544,128]{1,0:T(8,128)S(1)} %get-tuple-element.50.refs_3_, ...), custom_call_target="tpu_custom_call" | custom-call | flops 4000000000 | bytes 8000000 | tf_op jit(solution)/shard_map/forward/pallas_call | solution.py:432
  44.1 1.1 %forward.11 = f32[256,128]{1,0:T(8,128)S(1)} custom-call(s32[8,128]{1,0:T(8,128)S(4)} %get-tuple-element.60.slots, bf16[384,128]{1,0:T(8,128)(2,1)S(1)} %collective-permute-done.14.refs_0_, bf16[128,128]{1,0:T(8,128)(2,1)S(1)} %collective-permute-done.15.refs_1_, s32[544,128]{1,0:T(8,128)S(1)} %get-tuple-element.54.refs_2_, ...), custom_call_target="tpu_custom_call" | custom-call | flops 4000000000 | bytes 8000000 | tf_op jit(solution)/shard_map/forward/pallas_call | solution.py:432
  45.2 0.8 %collective-permute-start.17 = (f32[256,128]{1,0:T(8,128)S(1)}, f32[256,128]{1,0:T(8,128)S(1)}, u32[]{:S(2)}, u32[]{:S(2)}) collective-permute-start(f32[256,128]{1,0:T(8,128)S(1)} %forward.11), channel_id=1, source_target_pairs={{0,1},{1,0},{2,3},{3,2},{4,5},{5,4},{6,7},{7,6},{8,9},{9,8},{10,11... | collective-permute-start | bytes 393224 | tf_op jit(solution)/shard_map/ppermute | solution.py:447
  45.9 0.7 %forward.10.projection_ref = f32[256,128]{1,0:T(8,128)S(1)} custom-call(s32[8,128]{1,0:T(8,128)S(4)} %get-tuple-element.53.slots, bf16[384,128]{1,0:T(8,128)(2,1)S(1)} %collective-permute-done.14.refs_0_, bf16[128,128]{1,0:T(8,128)(2,1)S(1)} %collective-permute-done.15.refs_1_, s32[544,128]{1,0:T(8,128)S(1)} %get-tuple-element.54.refs_2_, ...), custom_call_target="tpu_custom_call" | custom-call | flops 4000000000 | bytes 8000000 | tf_op jit(solution)/shard_map/forward/pallas_call | solution.py:432
  48.3 0.9 %backward.11 = (bf16[256,128]{1,0:T(8,128)(2,1)S(1)}, bf16[256,128]{1,0:T(8,128)(2,1)S(1)}) custom-call(s32[8,128]{1,0:T(8,128)S(4)} %get-tuple-element.60.slots, bf16[256,128]{1,0:T(8,128)(2,1)S(1)} %collective-permute-done.18.refs_1_.refs_0_, s32[544,128]{1,0:T(8,128)S(1)} %get-tuple-element.64.refs_1_, f32[544,128]{1,0:T(8,128)S(1)} %get-tuple-element.65.refs_2_, ...), custom_call_target="tpu_custom_call" | custom-call | flops 4000000000 | bytes 8000000 | tf_op jit(solution)/shard_map/backward/pallas_call | solution.py:432
  49.2 1.2 %collective-permute-start.21 = (bf16[256,128]{1,0:T(8,128)(2,1)S(1)}, bf16[256,128]{1,0:T(8,128)(2,1)S(1)}, u32[]{:S(2)}, u32[]{:S(2)}) collective-permute-start(bf16[256,128]{1,0:T(8,128)(2,1)S(1)} %get-tuple-element.78), channel_id=1, source_target_pairs={{0,3},{1,4},{2,7},{3,0},{4,1},{5,6},{6,5},{7,2},{8,13},{9,10},{10,... | collective-permute-start | bytes 196616 | tf_op jit(solution)/shard_map/ppermute | solution.py:447
  51.0 1.5 %backward.9.sum_ref = f32[512,128]{1,0:T(8,128)S(1)} custom-call(s32[8,128]{1,0:T(8,128)S(4)} %get-tuple-element.47.slots, bf16[256,128]{1,0:T(8,128)(2,1)S(1)} %residual.3.refs_0_, bf16[256,128]{1,0:T(8,128)(2,1)S(1)} %collective-permute-done.18.refs_1_.refs_0_, s32[544,128]{1,0:T(8,128)S(1)} %get-tuple-element.61.refs_2_, ...), custom_call_target="tpu_custom_call" | custom-call | flops 4000000000 | bytes 8000000 | tf_op jit(solution)/shard_map/backward/pallas_call | solution.py:432
  53.0 1.0 %collective-permute-start.22 = (bf16[128,128]{1,0:T(8,128)(2,1)S(1)}, bf16[128,128]{1,0:T(8,128)(2,1)S(1)}, u32[]{:S(2)}, u32[]{:S(2)}) collective-permute-start(bf16[128,128]{1,0:T(8,128)(2,1)S(1)} %get-tuple-element.79), channel_id=1, source_target_pairs={{0,9},{1,2},{2,1},{3,10},{4,7},{5,12},{6,15},{7,4},{8,11},{9,0},{1... | collective-permute-start | bytes 98312 | tf_op jit(solution)/shard_map/ppermute | solution.py:447
  54.0 1.7 %collective-permute-start.23 = (bf16[128,128]{1,0:T(8,128)(2,1)S(1)}, bf16[128,128]{1,0:T(8,128)(2,1)S(1)}, u32[]{:S(2)}, u32[]{:S(2)}) collective-permute-start(bf16[128,128]{1,0:T(8,128)(2,1)S(1)} %get-tuple-element.80), channel_id=1, source_target_pairs={{0,12},{1,11},{2,8},{3,15},{4,14},{5,9},{6,10},{7,13},{8,2},{9,5},... | collective-permute-start | bytes 98312 | tf_op jit(solution)/shard_map/ppermute | solution.py:447
  56.1 1.2 %collective-permute-done.22.refs_2_ = bf16[128,128]{1,0:T(8,128)(2,1)S(1)} collective-permute-done((bf16[128,128]{1,0:T(8,128)(2,1)S(1)}, bf16[128,128]{1,0:T(8,128)(2,1)S(1)}, u32[]{:S(2)}, u32[]{:S(2)}) %collective-permute-start.22) | collective-permute-done | bytes 32800 | tf_op jit(solution)/shard_map/ppermute | solution.py:447
  57.3 2.4 %collective-permute-done.23.refs_3_ = bf16[128,128]{1,0:T(8,128)(2,1)S(1)} collective-permute-done((bf16[128,128]{1,0:T(8,128)(2,1)S(1)}, bf16[128,128]{1,0:T(8,128)(2,1)S(1)}, u32[]{:S(2)}, u32[]{:S(2)}) %collective-permute-start.23) | collective-permute-done | bytes 32800 | tf_op jit(solution)/shard_map/ppermute | solution.py:447
  (54 shorter events, 9.0 us)
Async XLA Ops:
  1.1 9.3 %collective-permute-start = (bf16[160,128]{1,0:T(8,128)(2,1)S(1)}, bf16[160,128]{1,0:T(8,128)(2,1)S(1)}, u32[]{:S(2)}, u32[]{:S(2)}) collective-permute-start(bf16[160,128]{1,0:T(8,128)(2,1)S(1)} %get-tuple-element.44), channel_id=1, source_target_pairs={{0,9},{1,2},{2,1},{3,10},{4,7},{5,12},{6,15},{7,4},{8,11},{9,0},{1... | collective-permute-start | bytes 122888 | tf_op jit(solution)/shard_map/ppermute | solution.py:447
  4.6 5.8 %collective-permute-start.1 = (bf16[160,128]{1,0:T(8,128)(2,1)S(1)}, bf16[160,128]{1,0:T(8,128)(2,1)S(1)}, u32[]{:S(2)}, u32[]{:S(2)}) collective-permute-start(bf16[160,128]{1,0:T(8,128)(2,1)S(1)} %get-tuple-element.45), channel_id=1, source_target_pairs={{0,5},{1,8},{2,11},{3,6},{4,13},{5,0},{6,3},{7,14},{8,1},{9,12},{1... | collective-permute-start | bytes 122888 | tf_op jit(solution)/shard_map/ppermute | solution.py:447
  6.5 5.9 %collective-permute-start.2 = (bf16[160,128]{1,0:T(8,128)(2,1)S(1)}, bf16[160,128]{1,0:T(8,128)(2,1)S(1)}, u32[]{:S(2)}, u32[]{:S(2)}) collective-permute-start(bf16[160,128]{1,0:T(8,128)(2,1)S(1)} %get-tuple-element.46), channel_id=1, source_target_pairs={{0,12},{1,11},{2,8},{3,15},{4,14},{5,9},{6,10},{7,13},{8,2},{9,5},... | collective-permute-start | bytes 122888 | tf_op jit(solution)/shard_map/ppermute | solution.py:447
  6.5 9.2 %collective-permute-start.4 = (bf16[160,128]{1,0:T(8,128)(2,1)S(1)}, bf16[160,128]{1,0:T(8,128)(2,1)S(1)}, u32[]{:S(2)}, u32[]{:S(2)}) collective-permute-start(bf16[160,128]{1,0:T(8,128)(2,1)S(1)} %get-tuple-element.48), channel_id=1, source_target_pairs={{0,15},{1,14},{2,13},{3,12},{4,11},{5,10},{6,9},{7,8},{8,7},{9,6},... | collective-permute-start | bytes 122888 | tf_op jit(solution)/shard_map/ppermute | solution.py:447
  10.4 5.3 %collective-permute-start.3 = (bf16[480,128]{1,0:T(8,128)(2,1)S(1)}, bf16[480,128]{1,0:T(8,128)(2,1)S(1)}, u32[]{:S(2)}, u32[]{:S(2)}) collective-permute-start(bf16[480,128]{1,0:T(8,128)(2,1)S(1)} %join.2.refs_0_), channel_id=1, source_target_pairs={{0,3},{1,4},{2,7},{3,0},{4,1},{5,6},{6,5},{7,2},{8,13},{9,10},{10,... | collective-permute-start | bytes 368648 | tf_op jit(solution)/shard_map/ppermute | solution.py:447
  18.4 1.4 %collective-permute-start.5 = (f32[288,128]{1,0:T(8,128)S(1)}, f32[288,128]{1,0:T(8,128)S(1)}, u32[]{:S(2)}, u32[]{:S(2)}) collective-permute-start(f32[288,128]{1,0:T(8,128)S(1)} %forward.8), channel_id=1, source_target_pairs={{0,1},{1,0},{2,3},{3,2},{4,5},{5,4},{6,7},{7,6},{8,9},{9,8},{10,11... | collective-permute-start | bytes 442376 | tf_op jit(solution)/shard_map/ppermute | solution.py:447
  18.5 1.4 %copy-start.1 = (bf16[32,8,128]{2,1,0:T(8,128)(2,1)S(1)}, bf16[32,8,128]{2,1,0:T(8,128)(2,1)}, u32[]{:S(2)}) copy-start(bf16[32,8,128]{2,1,0:T(8,128)(2,1)} %param.7) | copy-start | bytes 196612
  19.9 1.3 %collective-permute-start.6 = (bf16[256,128]{1,0:T(8,128)(2,1)S(1)}, bf16[256,128]{1,0:T(8,128)(2,1)S(1)}, u32[]{:S(2)}, u32[]{:S(2)}) collective-permute-start(bf16[256,128]{1,0:T(8,128)(2,1)S(1)} %residual.2.refs_0_), channel_id=1, source_target_pairs={{0,1},{1,0},{2,3},{3,2},{4,5},{5,4},{6,7},{7,6},{8,9},{9,8},{10,11... | collective-permute-start | bytes 196616 | tf_op jit(solution)/shard_map/ppermute | solution.py:447
  22.2 4.3 %collective-permute-start.9 = (bf16[256,128]{1,0:T(8,128)(2,1)S(1)}, bf16[256,128]{1,0:T(8,128)(2,1)S(1)}, u32[]{:S(2)}, u32[]{:S(2)}) collective-permute-start(bf16[256,128]{1,0:T(8,128)(2,1)S(1)} %get-tuple-element.70), channel_id=1, source_target_pairs={{0,3},{1,4},{2,7},{3,0},{4,1},{5,6},{6,5},{7,2},{8,13},{9,10},{10,... | collective-permute-start | bytes 196616 | tf_op jit(solution)/shard_map/ppermute | solution.py:447
  24.5 5.2 %collective-permute-start.7 = (bf16[256,128]{1,0:T(8,128)(2,1)S(1)}, bf16[256,128]{1,0:T(8,128)(2,1)S(1)}, u32[]{:S(2)}, u32[]{:S(2)}) collective-permute-start(bf16[256,128]{1,0:T(8,128)(2,1)S(1)} %get-tuple-element.67), channel_id=1, source_target_pairs={{0,3},{1,4},{2,7},{3,0},{4,1},{5,6},{6,5},{7,2},{8,13},{9,10},{10,... | collective-permute-start | bytes 196616 | tf_op jit(solution)/shard_map/ppermute | solution.py:447
  26.4 4.6 %collective-permute-start.10 = (bf16[128,128]{1,0:T(8,128)(2,1)S(1)}, bf16[128,128]{1,0:T(8,128)(2,1)S(1)}, u32[]{:S(2)}, u32[]{:S(2)}) collective-permute-start(bf16[128,128]{1,0:T(8,128)(2,1)S(1)} %get-tuple-element.71), channel_id=1, source_target_pairs={{0,9},{1,2},{2,1},{3,10},{4,7},{5,12},{6,15},{7,4},{8,11},{9,0},{1... | collective-permute-start | bytes 98312 | tf_op jit(solution)/shard_map/ppermute | solution.py:447
  26.5 3.3 %copy-start.2 = (f32[256,4]{0,1:T(4,128)S(1)}, f32[256,4]{0,1:T(4,128)}, u32[]{:S(2)}) copy-start(f32[256,4]{0,1:T(4,128)} %param.13) | copy-start | bytes 12292
  26.5 3.3 %copy-start.3 = (f32[256,4]{0,1:T(4,128)S(1)}, f32[256,4]{0,1:T(4,128)}, u32[]{:S(2)}) copy-start(f32[256,4]{0,1:T(4,128)} %param.12) | copy-start | bytes 12292
  26.5 3.3 %copy-start.4 = (s32[256,4]{0,1:T(4,128)S(1)}, s32[256,4]{0,1:T(4,128)}, u32[]{:S(2)}) copy-start(s32[256,4]{0,1:T(4,128)} %param.9) | copy-start | bytes 12292
  26.6 6.1 %collective-permute-start.11 = (bf16[128,128]{1,0:T(8,128)(2,1)S(1)}, bf16[128,128]{1,0:T(8,128)(2,1)S(1)}, u32[]{:S(2)}, u32[]{:S(2)}) collective-permute-start(bf16[128,128]{1,0:T(8,128)(2,1)S(1)} %get-tuple-element.72), channel_id=1, source_target_pairs={{0,12},{1,11},{2,8},{3,15},{4,14},{5,9},{6,10},{7,13},{8,2},{9,5},... | collective-permute-start | bytes 98312 | tf_op jit(solution)/shard_map/ppermute | solution.py:447
  29.7 0.7 %copy-start.5 = (s32[16]{0:T(128)S(1)}, s32[16]{0:T(128)}, u32[]{:S(2)}) copy-start(s32[16]{0:T(128)} %param.11) | copy-start | bytes 196
  29.7 4.0 %copy-start = (f32[16,8,128]{2,1,0:T(8,128)S(1)}, f32[16,8,128]{2,1,0:T(8,128)}, u32[]{:S(2)}) copy-start(f32[16,8,128]{2,1,0:T(8,128)} %param.8) | copy-start | bytes 196612
  29.7 4.0 %collective-permute-start.8 = (bf16[128,128]{1,0:T(8,128)(2,1)S(1)}, bf16[128,128]{1,0:T(8,128)(2,1)S(1)}, u32[]{:S(2)}, u32[]{:S(2)}) collective-permute-start(bf16[128,128]{1,0:T(8,128)(2,1)S(1)} %get-tuple-element.69), channel_id=1, source_target_pairs={{0,5},{1,8},{2,11},{3,6},{4,13},{5,0},{6,3},{7,14},{8,1},{9,12},{1... | collective-permute-start | bytes 98312 | tf_op jit(solution)/shard_map/ppermute | solution.py:447
  33.7 5.3 %collective-permute-start.12 = (bf16[128,128]{1,0:T(8,128)(2,1)S(1)}, bf16[128,128]{1,0:T(8,128)(2,1)S(1)}, u32[]{:S(2)}, u32[]{:S(2)}) collective-permute-start(bf16[128,128]{1,0:T(8,128)(2,1)S(1)} %get-tuple-element.74.refs_0_), channel_id=1, source_target_pairs={{0,9},{1,2},{2,1},{3,10},{4,7},{5,12},{6,15},{7,4},{8,11},{9,0},{1... | collective-permute-start | bytes 98312 | tf_op jit(solution)/shard_map/ppermute | solution.py:447
  33.8 5.2 %collective-permute-start.13 = (bf16[128,128]{1,0:T(8,128)(2,1)S(1)}, bf16[128,128]{1,0:T(8,128)(2,1)S(1)}, u32[]{:S(2)}, u32[]{:S(2)}) collective-permute-start(bf16[128,128]{1,0:T(8,128)(2,1)S(1)} %get-tuple-element.74.refs_0_), channel_id=1, source_target_pairs={{0,5},{1,8},{2,11},{3,6},{4,13},{5,0},{6,3},{7,14},{8,1},{9,12},{1... | collective-permute-start | bytes 98312 | tf_op jit(solution)/shard_map/ppermute | solution.py:447
  35.8 5.8 %collective-permute-start.16 = (bf16[128,128]{1,0:T(8,128)(2,1)S(1)}, bf16[128,128]{1,0:T(8,128)(2,1)S(1)}, u32[]{:S(2)}, u32[]{:S(2)}) collective-permute-start(bf16[128,128]{1,0:T(8,128)(2,1)S(1)} %get-tuple-element.74.refs_0_), channel_id=1, source_target_pairs={{0,12},{1,11},{2,8},{3,15},{4,14},{5,9},{6,10},{7,13},{8,2},{9,5},... | collective-permute-start | bytes 98312 | tf_op jit(solution)/shard_map/ppermute | solution.py:447
  37.9 6.2 %collective-permute-start.15 = (bf16[128,128]{1,0:T(8,128)(2,1)S(1)}, bf16[128,128]{1,0:T(8,128)(2,1)S(1)}, u32[]{:S(2)}, u32[]{:S(2)}) collective-permute-start(bf16[128,128]{1,0:T(8,128)(2,1)S(1)} %get-tuple-element.74.refs_0_), channel_id=1, source_target_pairs={{0,15},{1,14},{2,13},{3,12},{4,11},{5,10},{6,9},{7,8},{8,7},{9,6},... | collective-permute-start | bytes 98312 | tf_op jit(solution)/shard_map/ppermute | solution.py:447
  39.0 5.0 %collective-permute-start.14 = (bf16[384,128]{1,0:T(8,128)(2,1)S(1)}, bf16[384,128]{1,0:T(8,128)(2,1)S(1)}, u32[]{:S(2)}, u32[]{:S(2)}) collective-permute-start(bf16[384,128]{1,0:T(8,128)(2,1)S(1)} %join.3.refs_0_), channel_id=1, source_target_pairs={{0,3},{1,4},{2,7},{3,0},{4,1},{5,6},{6,5},{7,2},{8,13},{9,10},{10,... | collective-permute-start | bytes 294920 | tf_op jit(solution)/shard_map/ppermute | solution.py:447
  45.2 1.7 %collective-permute-start.17 = (f32[256,128]{1,0:T(8,128)S(1)}, f32[256,128]{1,0:T(8,128)S(1)}, u32[]{:S(2)}, u32[]{:S(2)}) collective-permute-start(f32[256,128]{1,0:T(8,128)S(1)} %forward.11), channel_id=1, source_target_pairs={{0,1},{1,0},{2,3},{3,2},{4,5},{5,4},{6,7},{7,6},{8,9},{9,8},{10,11... | collective-permute-start | bytes 393224 | tf_op jit(solution)/shard_map/ppermute | solution.py:447
  46.9 1.3 %collective-permute-start.18 = (bf16[256,128]{1,0:T(8,128)(2,1)S(1)}, bf16[256,128]{1,0:T(8,128)(2,1)S(1)}, u32[]{:S(2)}, u32[]{:S(2)}) collective-permute-start(bf16[256,128]{1,0:T(8,128)(2,1)S(1)} %residual.3.refs_0_), channel_id=1, source_target_pairs={{0,1},{1,0},{2,3},{3,2},{4,5},{5,4},{6,7},{7,6},{8,9},{9,8},{10,11... | collective-permute-start | bytes 196616 | tf_op jit(solution)/shard_map/ppermute | solution.py:447
  49.2 3.8 %collective-permute-start.21 = (bf16[256,128]{1,0:T(8,128)(2,1)S(1)}, bf16[256,128]{1,0:T(8,128)(2,1)S(1)}, u32[]{:S(2)}, u32[]{:S(2)}) collective-permute-start(bf16[256,128]{1,0:T(8,128)(2,1)S(1)} %get-tuple-element.78), channel_id=1, source_target_pairs={{0,3},{1,4},{2,7},{3,0},{4,1},{5,6},{6,5},{7,2},{8,13},{9,10},{10,... | collective-permute-start | bytes 196616 | tf_op jit(solution)/shard_map/ppermute | solution.py:447
  50.5 5.2 %collective-permute-start.19 = (bf16[256,128]{1,0:T(8,128)(2,1)S(1)}, bf16[256,128]{1,0:T(8,128)(2,1)S(1)}, u32[]{:S(2)}, u32[]{:S(2)}) collective-permute-start(bf16[256,128]{1,0:T(8,128)(2,1)S(1)} %get-tuple-element.75), channel_id=1, source_target_pairs={{0,3},{1,4},{2,7},{3,0},{4,1},{5,6},{6,5},{7,2},{8,13},{9,10},{10,... | collective-permute-start | bytes 196616 | tf_op jit(solution)/shard_map/ppermute | solution.py:447
  53.0 4.3 %collective-permute-start.22 = (bf16[128,128]{1,0:T(8,128)(2,1)S(1)}, bf16[128,128]{1,0:T(8,128)(2,1)S(1)}, u32[]{:S(2)}, u32[]{:S(2)}) collective-permute-start(bf16[128,128]{1,0:T(8,128)(2,1)S(1)} %get-tuple-element.79), channel_id=1, source_target_pairs={{0,9},{1,2},{2,1},{3,10},{4,7},{5,12},{6,15},{7,4},{8,11},{9,0},{1... | collective-permute-start | bytes 98312 | tf_op jit(solution)/shard_map/ppermute | solution.py:447
  54.0 5.7 %collective-permute-start.23 = (bf16[128,128]{1,0:T(8,128)(2,1)S(1)}, bf16[128,128]{1,0:T(8,128)(2,1)S(1)}, u32[]{:S(2)}, u32[]{:S(2)}) collective-permute-start(bf16[128,128]{1,0:T(8,128)(2,1)S(1)} %get-tuple-element.80), channel_id=1, source_target_pairs={{0,12},{1,11},{2,8},{3,15},{4,14},{5,9},{6,10},{7,13},{8,2},{9,5},... | collective-permute-start | bytes 98312 | tf_op jit(solution)/shard_map/ppermute | solution.py:447
  55.7 4.0 %collective-permute-start.20 = (bf16[128,128]{1,0:T(8,128)(2,1)S(1)}, bf16[128,128]{1,0:T(8,128)(2,1)S(1)}, u32[]{:S(2)}, u32[]{:S(2)}) collective-permute-start(bf16[128,128]{1,0:T(8,128)(2,1)S(1)} %get-tuple-element.77), channel_id=1, source_target_pairs={{0,5},{1,8},{2,11},{3,6},{4,13},{5,0},{6,3},{7,14},{8,1},{9,12},{1... | collective-permute-start | bytes 98312 | tf_op jit(solution)/shard_map/ppermute | solution.py:447
